TPU v7x, 128 devices: a whole 4x4x4 slice. The times are simulated.
128 devices in a mesh: grp: 8 (over z, y_lo), blk: 16 (over x, y_hi, core).
Axes of the slice: x: 4, y: 4 (y_hi: 2, y_lo: 2; y = y_hi * 2 + y_lo), z: 4, core: 2. Of those that a mesh axis runs over, the one named last changes fastest.
Arguments:
- query: bfloat16 [16, 1024, 12288], P('blk', 'grp'), may hold values from -12 to 12
- latent: bfloat16 [16, 1024, 576], P('blk', 'grp'), may hold values from -12 to 12
- positions: int32 [16, 1024], P('blk'), may hold values from 0 to 255, as said below
- key_up: bfloat16 [512, 8192], P(None, 'grp'), may hold values from -0.25 to 0.25
- value_up: bfloat16 [512, 8192], P(None, 'grp'), may hold values from -0.25 to 0.25
- grad_out: bfloat16 [16, 1024, 8192], P('blk', None, 'grp'), may hold values from -6 to 6
Outputs:
- grad_query: bfloat16 [16, 1024, 12288], P('blk', None, 'grp')
- grad_latent: bfloat16 [16, 1024, 576], P('blk', 'grp')
Inputs may be any that keep to these rules, and one draw needn't show every extreme that they name: positions[b, t] is the number of tokens that precede token t of group b in its document; documents are runs of consecutive tokens of the whole sequence, group after group; each has at most 256 tokens, and every one but the last of the sequence has at least 64.
All inputs are finite; a program needn't handle non-finite values.
Results may differ from a plain program's by a relative error of at most 0.02.
The roundings to bfloat16 on the way count: a program that leaves them out, or rounds other values in their place, can miss the bound.
Values may be sent and summed in bfloat16 or wider, within the bound.
A program may use at most 192 MiB of HBM per device.

v0:
```python
import math

import jax
import jax.numpy as jnp
from jax import lax
from jax.sharding import PartitionSpec as P

D_C = 512
D_R = 64
D_N = 128
D_V = 128


rope_base = 10000.0
yarn_factor = 40.0
pretrain_context = 4096.0


def from_behind(block, axis, distance):
    devices = range(lax.axis_size(axis))
    route = [(i - distance, i) for i in devices if i - distance in devices]
    return lax.ppermute(block, axis, route)


def yarn_freqs(width):
    half_width = width // 2
    freq_index = jnp.arange(half_width, dtype=jnp.float32)
    extrapolated = rope_base ** (-2.0 * freq_index / width)
    lowest = max(
        math.floor(
            width * math.log(pretrain_context / (64.0 * math.pi)) / (2.0 * math.log(rope_base))
        ),
        0,
    )
    highest = min(
        math.ceil(
            width * math.log(pretrain_context / (2.0 * math.pi)) / (2.0 * math.log(rope_base))
        ),
        width - 1,
    )
    ramp_up = jnp.clip((freq_index - lowest) / (highest - lowest), 0.0, 1.0)
    return extrapolated / yarn_factor * ramp_up + extrapolated * (1.0 - ramp_up)


def rotate(vectors, cos_table, sin_table, direction):
    half_width = vectors.shape[-1] // 2
    first_half = vectors[..., :half_width]
    second_half = vectors[..., half_width:]
    return jnp.concatenate(
        [
            first_half * cos_table - direction * second_half * sin_table,
            second_half * cos_table + direction * first_half * sin_table,
        ],
        axis=-1,
    )


def add_span(total, addend, first_row):
    current = lax.dynamic_slice_in_dim(total, first_row, addend.shape[0], 0)
    return lax.dynamic_update_slice_in_dim(total, current + addend, first_row, 0)


def per_device(query, latent, positions, key_up, value_up, grad_out):
    tok_dev = query.shape[1]
    group_tok = tok_dev * lax.axis_size("grp")
    doc_max = 2 * tok_dev
    tail_start = group_tok - doc_max
    head_dev = key_up.shape[1] // D_N
    mscale = 0.1 * math.log(yarn_factor) + 1.0
    scaling = (D_N + D_R) ** (-0.5) * mscale * mscale
    group_pos = positions[0]
    angles = group_pos.astype(jnp.float32)[:, None] * yarn_freqs(D_R)[None, :]
    cos_table = jnp.cos(angles)
    sin_table = jnp.sin(angles)
    own_start = lax.axis_index("grp") * tok_dev
    own_cos = lax.dynamic_slice_in_dim(cos_table, own_start, tok_dev, 0)
    own_sin = lax.dynamic_slice_in_dim(sin_table, own_start, tok_dev, 0)
    own_rot = rotate(latent[0, :, D_C:].astype(jnp.float32), own_cos, own_sin, 1.0).astype(
        jnp.bfloat16
    )
    own_piece = jnp.concatenate([latent[0, :, :D_C], own_rot], axis=1)
    rows_piece = lax.all_gather(own_piece, "grp", axis=0, tiled=True)
    compressed = rows_piece[:, :D_C]
    keys_piece = jnp.dot(compressed, key_up, preferred_element_type=jnp.float32).astype(
        jnp.bfloat16
    )
    values_piece = jnp.dot(compressed, value_up, preferred_element_type=jnp.float32).astype(
        jnp.bfloat16
    )
    query_heads = lax.all_to_all(query[0], "grp", split_axis=1, concat_axis=0, tiled=True)
    rot_own = rows_piece[:, D_C:]
    keys_earlier, values_earlier, rot_earlier = from_behind(
        (keys_piece[tail_start:], values_piece[tail_start:], rot_own[tail_start:]), "blk", 1
    )
    key_rows = doc_max + group_tok
    keys_all = jnp.concatenate([keys_earlier, keys_piece], axis=0).reshape(key_rows, head_dev, D_N)
    values_all = jnp.concatenate([values_earlier, values_piece], axis=0).reshape(
        key_rows, head_dev, D_V
    )
    rot_all = jnp.concatenate([rot_earlier, rot_own], axis=0)
    query_group = query_heads.reshape(group_tok, head_dev, D_N + D_R)
    query_nope = query_group[..., :D_N]
    query_rot = rotate(
        query_group[..., D_N:].astype(jnp.float32),
        cos_table[:, None, :],
        sin_table[:, None, :],
        1.0,
    ).astype(jnp.bfloat16)
    grad_heads = grad_out[0].reshape(group_tok, head_dev, D_V)
    row_count = min(512, group_tok)
    key_span = doc_max + row_count

    def attend_block(totals, block_id):
        keys_acc, values_acc, rot_acc = totals
        first_row = block_id * row_count
        block_nope = lax.dynamic_slice_in_dim(query_nope, first_row, row_count, 0)
        block_rot = lax.dynamic_slice_in_dim(query_rot, first_row, row_count, 0)
        block_grad = lax.dynamic_slice_in_dim(grad_heads, first_row, row_count, 0)
        block_pos = lax.dynamic_slice_in_dim(group_pos, first_row, row_count, 0)
        span_keys = lax.dynamic_slice_in_dim(keys_all, first_row, key_span, 0)
        span_values = lax.dynamic_slice_in_dim(values_all, first_row, key_span, 0)
        span_rot = lax.dynamic_slice_in_dim(rot_all, first_row, key_span, 0)
        row_ids = first_row + jnp.arange(row_count, dtype=jnp.int32)
        col_ids = first_row + jnp.arange(key_span, dtype=jnp.int32)
        visible = (col_ids[None, :] >= doc_max + row_ids[:, None] - block_pos[:, None]) & (
            col_ids[None, :] <= doc_max + row_ids[:, None]
        )
        scores = jnp.einsum(
            "rhd,khd->hrk", block_nope, span_keys, preferred_element_type=jnp.float32
        )
        scores = (
            scores
            + jnp.einsum("rhd,kd->hrk", block_rot, span_rot, preferred_element_type=jnp.float32)
        ) * scaling
        scores = jnp.where(visible[None], scores, -jnp.inf)
        top_score = jnp.max(scores, axis=-1, keepdims=True)
        weights = jnp.exp(scores - top_score)
        attention = weights / jnp.sum(weights, axis=-1, keepdims=True)
        attention_low = attention.astype(jnp.bfloat16)
        grad_probs = jnp.einsum(
            "rhd,khd->hrk", block_grad, span_values, preferred_element_type=jnp.float32
        )
        delta_rows = jnp.sum(attention * grad_probs, axis=-1, keepdims=True)
        grad_scores = (attention * (grad_probs - delta_rows) * scaling).astype(jnp.bfloat16)
        grad_nope = jnp.einsum(
            "hrk,khd->rhd", grad_scores, span_keys, preferred_element_type=jnp.float32
        )
        grad_rot = jnp.einsum(
            "hrk,kd->rhd", grad_scores, span_rot, preferred_element_type=jnp.float32
        )
        keys_part = jnp.einsum(
            "hrk,rhd->khd", grad_scores, block_nope, preferred_element_type=jnp.float32
        )
        values_part = jnp.einsum(
            "hrk,rhd->khd", attention_low, block_grad, preferred_element_type=jnp.float32
        )
        rot_part = jnp.einsum(
            "hrk,rhd->kd", grad_scores, block_rot, preferred_element_type=jnp.float32
        )
        keys_acc = add_span(keys_acc, keys_part, first_row)
        values_acc = add_span(values_acc, values_part, first_row)
        rot_acc = add_span(rot_acc, rot_part, first_row)
        return ((keys_acc, values_acc, rot_acc), (grad_nope, grad_rot))

    initial = (
        jnp.zeros((key_rows, head_dev, D_N), jnp.float32),
        jnp.zeros((key_rows, head_dev, D_V), jnp.float32),
        jnp.zeros((key_rows, D_R), jnp.float32),
    )
    totals, rows_out = lax.scan(
        attend_block, initial, jnp.arange(group_tok // row_count, dtype=jnp.int32)
    )
    keys_total, values_total, rot_total = totals
    nope_rows, rot_rows = rows_out
    grad_rot = rotate(
        rot_rows.reshape(group_tok, head_dev, D_R),
        cos_table[:, None, :],
        sin_table[:, None, :],
        -1.0,
    )
    grad_query = jnp.concatenate(
        [nope_rows.reshape(group_tok, head_dev, D_N), grad_rot], axis=-1
    ).astype(jnp.bfloat16)
    grad_query = grad_query.reshape(1, group_tok, head_dev * (D_N + D_R))
    key_low = keys_total.astype(jnp.bfloat16).reshape(key_rows, head_dev * D_N)
    value_low = values_total.astype(jnp.bfloat16).reshape(key_rows, head_dev * D_V)
    contract = (((1,), (1,)), ((), ()))
    projected = lax.dot_general(key_low, key_up, contract, preferred_element_type=jnp.float32)
    projected = projected + lax.dot_general(
        value_low, value_up, contract, preferred_element_type=jnp.float32
    )
    partial_value = jnp.concatenate([projected, rot_total], axis=1)
    earlier_part = partial_value[:doc_max]
    own_part = partial_value[doc_max:]
    leading = jnp.zeros((tail_start, D_C + D_R), jnp.float32)
    returned = from_behind(earlier_part, "blk", -1)
    summed = lax.psum_scatter(
        own_part + jnp.concatenate([leading, returned], axis=0),
        "grp",
        scatter_dimension=0,
        tiled=True,
    )
    rope_grad = rotate(summed[:, D_C:], own_cos, own_sin, -1.0)
    grad_latent = jnp.concatenate([summed[:, :D_C], rope_grad], axis=1).astype(jnp.bfloat16)
    return (grad_query, grad_latent[None])


def solution(mesh):
    placed = (
        P("blk", "grp", None),
        P("blk", "grp", None),
        P("blk", None),
        P(None, "grp"),
        P(None, "grp"),
        P("blk", None, "grp"),
    )
    return jax.shard_map(
        per_device,
        mesh=mesh,
        in_specs=placed,
        out_specs=(P("blk", None, "grp"), P("blk", "grp", None)),
        check_vma=False,
    )
```

profile of v0, /device:TPU:6, one launch (start us, length us, event | category | flops | bytes accessed | tf_op | source)
XLA Modules:
  0.0 688.9 jit_solution(7376352552890882075)
XLA Ops:
  11.6 4.6 copy.58
  16.3 6.3 all-to-all-start
  22.6 48.9 %all-gather.2.cloned.1.call-done = bf16[1024,576]{0,1:T(8,128)(2,1)} async-done(((bf16[128,576]{0,1:T(8,128)(2,1)}), bf16[1024,576]{0,1:T(8,128)(2,1)}) %all-gather.2.cloned.1.call-update) | async-done | bytes 1179664 | tf_op jit(solution)/shard_map/all_gather | solution.py:82
  80.3 4.3 collective-permute-start.2
  87.5 4.0 copy.60
  103.8 10.7 %copy.59 = bf16[8,128,1536]{1,0,2:T(8,128)(2,1)} copy(bf16[8,128,1536]{1,2,0:T(8,128)(2,1)} %bitcast.11) | data formatting | bytes 6291456 | tf_op jit(solution)/shard_map/all_to_all | solution.py:90
  114.5 5.8 reshape.226
  131.8 467.9 %while.18 = (s32[]{:T(128)}, f32[1280,8,128]{0,2,1:T(8,128)}, f32[1280,8,128]{0,2,1:T(8,128)}, f32[1280,64]{0,1:T(8,128)S(1)}, bf16[2,512,8,128]{3,2,1,0:T(8,128...) while((s32[]{:T(128)}, f32[1280,8,128]{0,2,1:T(8,128)}, ...), condition=%wide.region_4.5_spmd, body=%wide.region_0.4_spmd.sunk | while | flops 5350566912 | bytes 330924928 | solution.py:170
  159.8 6.7 fusion.139
  166.6 15.1 %fusion.140 = (f32[8,512]{1,0:T(8,128)S(1)}, f32[8,512,768]{2,1,0:T(8,128)}) fusion(f32[8,512,768]{2,1,0:T(8,128)} %fusion.139), kind=kOutput, calls=%fused_computation.103.clone.1 | output fusion | flops 6292223 | bytes 25182208 | tf_op jit(solution)/shard_map/while/body/eval_jaxpr/sub | solution.py:137
  181.6 8.1 %fusion.137 = f32[8,512,768]{2,1,0:T(8,128)} fusion(bf16[768,8,128]{2,1,0:T(8,128)(2,1)} %get-tuple-element.281, bf16[1024,8,128]{0,2,1:T(8,128)(2,1)} %get-tuple-element.337, s32[]{:T(128)S(6)} %select_n.32), kind=kOutput, calls=%fused_computation.21.clone.1 | convolution fusion | flops 805306368 | bytes 15204356 | tf_op jit(solution)/shard_map/while/body/eval_jaxpr/rhd,khd->hrk/dot_general | solution.py:140
  189.8 32.3 %fusion.145 = f32[1,512,8,64]{1,3,2,0:T(8,128)} fusion(f32[8,512,768]{2,1,0:T(8,128)} %fusion.137, bf16[1280,64]{0,1:T(8,128)(2,1)S(1)} %get-tuple-element.335, s32[]{:T(128)S(6)} %select_n.16, f32[8,512,768]{2,1,0:T(8,128)} %get-tuple-element.285, f32[8,512]{1,0:T(8,128)S(1)} %get-tuple-element.286), kind=kOutput, calls=%fused_computation.27.clone.1 | convolution fusion | flops 424678144 | bytes 51511300 | tf_op jit(solution)/shard_map/while/body/eval_jaxpr/hrk,kd->rhd/dot_general | solution.py:148
  225.3 19.6 %dynamic_update_slice.30 = f32[2,512,8,64]{1,0,3,2:T(2,128)} dynamic-update-slice(f32[2,512,8,64]{1,0,3,2:T(2,128)} %get-tuple-element.311, f32[1,512,8,64]{1,0,3,2:T(1,128)} %copy.101, s32[]{:T(128)} %get-tuple-element.306, s32[]{:T(128)} %constant.11.clone.1..sunk, s32[]{:T(128)} %constant.11.clone.1..sunk, s32[]{:T(128)} %constant.11.clone.1..sunk) | dynamic-update-slice | bytes 2097156 | tf_op jit(solution)/shard_map/while/body/jit(dynamic_update_index_in_dim)/dynamic_update_slice | solution.py:170
  245.0 41.3 %fusion.144 = bf16[1,512,8,128]{1,3,2,0:T(8,128)(2,1)} fusion(f32[8,512,768]{2,1,0:T(8,128)} %fusion.137, bf16[768,8,128]{2,1,0:T(8,128)(2,1)S(1)} %get-tuple-element.282, f32[8,512,768]{2,1,0:T(8,128)} %get-tuple-element.285, f32[8,512]{1,0:T(8,128)S(1)} %get-tuple-element.286), kind=kOutput, calls=%fused_computation.20.clone.1 | convolution fusion | flops 827331328 | bytes 27803648 | tf_op jit(solution)/shard_map/while/body/eval_jaxpr/hrk,khd->rhd/dot_general | solution.py:145
  289.0 31.5 %fusion.143 = f32[1280,64]{0,1:T(8,128)S(1)} fusion(f32[1280,64]{0,1:T(8,128)S(1)} %get-tuple-element.309, s32[]{:T(128)S(6)} %select_n.16, f32[8,512,768]{2,1,0:T(8,128)} %fusion.137, bf16[1024,8,64]{0,2,1:T(8,128)(2,1)} %get-tuple-element.336, s32[]{:T(128)S(6)} %select_n.32, f32[8,512,768]{2,1,0:T(8,128)} %get-tuple-element.285, ...), kind=kOutput, calls=%fused_computation.30.clone.1 | convolution fusion | flops 424727296 | bytes 51281928 | tf_op jit(solution)/shard_map/while/body/eval_jaxpr/hrk,rhd->kd/dot_general | solution.py:157
  320.5 17.2 %fusion.142 = f32[1280,8,128]{0,2,1:T(8,128)} fusion(f32[1280,8,128]{0,2,1:T(8,128)} %get-tuple-element.308, s32[]{:T(128)S(6)} %select_n.16, bf16[1024,8,128]{0,2,1:T(8,128)(2,1)S(1)} %copy-done.1, s32[]{:T(128)S(6)} %select_n.32, f32[8,512]{1,0:T(8,128)S(1)} %get-tuple-element.286, f32[8,512,768]{2,1,0:T(8,128)} %fusion.139), kind=kOutput, calls=%fused_computation.17.clone.1 | convolution fusion | flops 815534848 | bytes 32522248 | tf_op jit(solution)/shard_map/while/body/eval_jaxpr/hrk,rhd->khd/dot_general | solution.py:154
  337.7 35.1 %fusion.141 = f32[1280,8,128]{0,2,1:T(8,128)} fusion(f32[1280,8,128]{0,2,1:T(8,128)} %get-tuple-element.307, s32[]{:T(128)S(6)} %select_n.16, f32[8,512,768]{2,1,0:T(8,128)} %fusion.137, bf16[1024,8,128]{0,2,1:T(8,128)(2,1)} %get-tuple-element.332, s32[]{:T(128)S(6)} %select_n.32, f32[8,512,768]{2,1,0:T(8,128)} %get-tuple-element.285, ...), kind=kOutput, calls=%fused_computation.19.clone.1 | convolution fusion | flops 828117760 | bytes 57704456 | tf_op jit(solution)/shard_map/while/body/eval_jaxpr/hrk,rhd->khd/dot_general | solution.py:151
  380.9 6.7 fusion.139
  387.7 15.1 %fusion.140 = (f32[8,512]{1,0:T(8,128)S(1)}, f32[8,512,768]{2,1,0:T(8,128)}) fusion(f32[8,512,768]{2,1,0:T(8,128)} %fusion.139), kind=kOutput, calls=%fused_computation.103.clone.1 | output fusion | flops 6292223 | bytes 25182208 | tf_op jit(solution)/shard_map/while/body/eval_jaxpr/sub | solution.py:137
  402.8 8.1 %fusion.137 = f32[8,512,768]{2,1,0:T(8,128)} fusion(bf16[768,8,128]{2,1,0:T(8,128)(2,1)} %get-tuple-element.281, bf16[1024,8,128]{0,2,1:T(8,128)(2,1)} %get-tuple-element.337, s32[]{:T(128)S(6)} %select_n.32), kind=kOutput, calls=%fused_computation.21.clone.1 | convolution fusion | flops 805306368 | bytes 15204356 | tf_op jit(solution)/shard_map/while/body/eval_jaxpr/rhd,khd->hrk/dot_general | solution.py:140
  410.9 32.3 %fusion.145 = f32[1,512,8,64]{1,3,2,0:T(8,128)} fusion(f32[8,512,768]{2,1,0:T(8,128)} %fusion.137, bf16[1280,64]{0,1:T(8,128)(2,1)S(1)} %get-tuple-element.335, s32[]{:T(128)S(6)} %select_n.16, f32[8,512,768]{2,1,0:T(8,128)} %get-tuple-element.285, f32[8,512]{1,0:T(8,128)S(1)} %get-tuple-element.286), kind=kOutput, calls=%fused_computation.27.clone.1 | convolution fusion | flops 424678144 | bytes 51511300 | tf_op jit(solution)/shard_map/while/body/eval_jaxpr/hrk,kd->rhd/dot_general | solution.py:148
  446.5 19.6 %dynamic_update_slice.30 = f32[2,512,8,64]{1,0,3,2:T(2,128)} dynamic-update-slice(f32[2,512,8,64]{1,0,3,2:T(2,128)} %get-tuple-element.311, f32[1,512,8,64]{1,0,3,2:T(1,128)} %copy.101, s32[]{:T(128)} %get-tuple-element.306, s32[]{:T(128)} %constant.11.clone.1..sunk, s32[]{:T(128)} %constant.11.clone.1..sunk, s32[]{:T(128)} %constant.11.clone.1..sunk) | dynamic-update-slice | bytes 2097156 | tf_op jit(solution)/shard_map/while/body/jit(dynamic_update_index_in_dim)/dynamic_update_slice | solution.py:170
  466.1 41.3 %fusion.144 = bf16[1,512,8,128]{1,3,2,0:T(8,128)(2,1)} fusion(f32[8,512,768]{2,1,0:T(8,128)} %fusion.137, bf16[768,8,128]{2,1,0:T(8,128)(2,1)S(1)} %get-tuple-element.282, f32[8,512,768]{2,1,0:T(8,128)} %get-tuple-element.285, f32[8,512]{1,0:T(8,128)S(1)} %get-tuple-element.286), kind=kOutput, calls=%fused_computation.20.clone.1 | convolution fusion | flops 827331328 | bytes 27803648 | tf_op jit(solution)/shard_map/while/body/eval_jaxpr/hrk,khd->rhd/dot_general | solution.py:145
  510.2 31.4 %fusion.143 = f32[1280,64]{0,1:T(8,128)S(1)} fusion(f32[1280,64]{0,1:T(8,128)S(1)} %get-tuple-element.309, s32[]{:T(128)S(6)} %select_n.16, f32[8,512,768]{2,1,0:T(8,128)} %fusion.137, bf16[1024,8,64]{0,2,1:T(8,128)(2,1)} %get-tuple-element.336, s32[]{:T(128)S(6)} %select_n.32, f32[8,512,768]{2,1,0:T(8,128)} %get-tuple-element.285, ...), kind=kOutput, calls=%fused_computation.30.clone.1 | convolution fusion | flops 424727296 | bytes 51281928 | tf_op jit(solution)/shard_map/while/body/eval_jaxpr/hrk,rhd->kd/dot_general | solution.py:157
  541.6 17.2 %fusion.142 = f32[1280,8,128]{0,2,1:T(8,128)} fusion(f32[1280,8,128]{0,2,1:T(8,128)} %get-tuple-element.308, s32[]{:T(128)S(6)} %select_n.16, bf16[1024,8,128]{0,2,1:T(8,128)(2,1)S(1)} %copy-done.1, s32[]{:T(128)S(6)} %select_n.32, f32[8,512]{1,0:T(8,128)S(1)} %get-tuple-element.286, f32[8,512,768]{2,1,0:T(8,128)} %fusion.139), kind=kOutput, calls=%fused_computation.17.clone.1 | convolution fusion | flops 815534848 | bytes 32522248 | tf_op jit(solution)/shard_map/while/body/eval_jaxpr/hrk,rhd->khd/dot_general | solution.py:154
  558.8 35.2 %fusion.141 = f32[1280,8,128]{0,2,1:T(8,128)} fusion(f32[1280,8,128]{0,2,1:T(8,128)} %get-tuple-element.307, s32[]{:T(128)S(6)} %select_n.16, f32[8,512,768]{2,1,0:T(8,128)} %fusion.137, bf16[1024,8,128]{0,2,1:T(8,128)(2,1)} %get-tuple-element.332, s32[]{:T(128)S(6)} %select_n.32, f32[8,512,768]{2,1,0:T(8,128)} %get-tuple-element.285, ...), kind=kOutput, calls=%fused_computation.19.clone.1 | convolution fusion | flops 828117760 | bytes 57704456 | tf_op jit(solution)/shard_map/while/body/eval_jaxpr/hrk,rhd->khd/dot_general | solution.py:151
  610.3 7.4 %collective-permute-done.3 = f32[256,576]{0,1:T(8,128)S(1)} collective-permute-done((f32[256,576]{0,1:T(8,128)S(1)}, f32[256,576]{0,1:T(8,128)S(1)}, u32[]{:S(2)}, u32[]{:S(2)}) %collective-permute-start.3) | collective-permute-done | bytes 589856 | tf_op jit(solution)/shard_map/ppermute | solution.py:22
  627.4 3.4 copy.68
  630.8 4.9 pad_maximum_fusion
  635.7 6.5 copy.69
  642.2 4.6 copy.70
  646.8 32.6 %reduce-scatter.2.cloned.1.call-done = f32[128,576]{0,1:T(8,128)} async-done(((f32[1024,576]{0,1:T(8,128)}), f32[128,576]{0,1:T(8,128)}) %reduce-scatter.2.cloned.1.call-update) | async-done | bytes 294928 | tf_op jit(solution)/shard_map/reduce_scatter | solution.py:197
  (103 shorter events, 89.5 us)
Async XLA Ops:
  7.2 64.4 %copy-start = (bf16[512,1024]{1,0:T(8,128)(2,1)S(1)}, bf16[512,1024]{1,0:T(8,128)(2,1)}, u32[]{:S(2)}) copy-start(bf16[512,1024]{1,0:T(8,128)(2,1)} %param.11) | copy-start | bytes 3145732
  7.2 64.4 %all-gather.2.cloned.1.call-start = ((), (), s32[]{:S(2)}) async-start(), calls=%async_computation.2 | async-start | bytes 1327104 | tf_op jit(solution)/shard_map/all_gather | solution.py:82
  10.9 114.0 %copy-start.6 = (f32[1024,32]{0,1:T(8,128)}, f32[1024,32]{0,1:T(8,128)S(1)}, u32[]{:S(2)}) copy-start(f32[1024,32]{0,1:T(8,128)S(1)} %get-tuple-element.189) | copy-start | bytes 393220
  10.9 114.0 %copy-start.7 = (f32[1024,32]{0,1:T(8,128)}, f32[1024,32]{0,1:T(8,128)S(1)}, u32[]{:S(2)}) copy-start(f32[1024,32]{0,1:T(8,128)S(1)} %get-tuple-element.188) | copy-start | bytes 393220
  16.3 87.5 %all-to-all-start = ((bf16[128,8,1536]{0,2,1:T(8,128)(2,1)}), bf16[128,8,1536]{0,2,1:T(8,128)(2,1)}, u32[]{:S(2)}, u32[]{:S(2)}) async-start(bf16[128,8,1536]{0,2,1:T(8,128)(2,1)} %bitcast.99), calls=%async_computation | async-start | bytes 6291456 | tf_op jit(solution)/shard_map/all_to_all | solution.py:90
  22.6 656.8 %reduce-scatter.2.cloned.1.call-start = ((), (), s32[]{:S(2)}) async-start(), calls=%async_computation.3 | async-start | bytes 2654208 | tf_op jit(solution)/shard_map/reduce_scatter | solution.py:197
  71.5 5.4 copy-start.8
  74.2 5.3 copy-start.3
  75.0 20.6 %collective-permute-start = (bf16[256,1024]{1,0:T(8,128)(2,1)}, bf16[256,1024]{1,0:T(8,128)(2,1)}, u32[]{:S(2)}, u32[]{:S(2)}) collective-permute-start(bf16[256,1024]{1,0:T(8,128)(2,1)} %slice.89), channel_id=1, source_target_pairs={{0,1},{1,2},{2,3},{3,4},{4,5},{5,6},{6,7},{7,8},{8,9},{9,10},{10,1... | collective-permute-start | bytes 1572872 | tf_op jit(solution)/shard_map/ppermute | solution.py:22
  79.5 14.7 %slice-start.2 = ((bf16[1024,576]{0,1:T(8,128)(2,1)}), bf16[1024,64]{0,1:T(8,128)(2,1)S(1)}, s32[]{:S(2)}) async-start(bf16[1024,576]{0,1:T(8,128)(2,1)} %all-gather.2.cloned.1.call-done), calls=%async_computation.6 | async-start | bytes 262144 | tf_op jit(solution)/shard_map/slice | solution.py:91
  80.3 19.7 %collective-permute-start.2 = (bf16[256,1024]{1,0:T(8,128)(2,1)}, bf16[256,1024]{1,0:T(8,128)(2,1)}, u32[]{:S(2)}, u32[]{:S(2)}) collective-permute-start(bf16[256,1024]{1,0:T(8,128)(2,1)} %slice.95), channel_id=1, source_target_pairs={{0,1},{1,2},{2,3},{3,4},{4,5},{5,6},{6,7},{7,8},{8,9},{9,10},{10,1... | collective-permute-start | bytes 1572872 | tf_op jit(solution)/shard_map/ppermute | solution.py:22
  85.2 9.0 %collective-permute-start.1 = (bf16[256,64]{0,1:T(8,128)(2,1)}, bf16[256,64]{0,1:T(8,128)(2,1)}, u32[]{:S(2)}, u32[]{:S(2)}) collective-permute-start(bf16[256,64]{0,1:T(8,128)(2,1)} %slice.90), channel_id=1, source_target_pairs={{0,1},{1,2},{2,3},{3,4},{4,5},{5,6},{6,7},{7,8},{8,9},{9,10},{10,1... | collective-permute-start | bytes 98312 | tf_op jit(solution)/shard_map/ppermute | solution.py:22
  126.3 5.5 copy-start.4
  126.3 5.5 copy-start.9
  156.2 3.6 copy-start.2
  289.0 31.5 %copy-start.1 = (bf16[1024,8,128]{0,2,1:T(8,128)(2,1)S(1)}, bf16[1024,8,128]{0,2,1:T(8,128)(2,1)}, u32[]{:S(2)}) copy-start(bf16[1024,8,128]{0,2,1:T(8,128)(2,1)} %get-tuple-element.337) | copy-start | bytes 6291460 | tf_op jit(solution)/shard_map/while
  337.7 35.1 %copy-start.5 = (bf16[1280,64]{0,1:T(8,128)(2,1)S(1)}, bf16[1280,64]{0,1:T(8,128)(2,1)}, u32[]{:S(2)}) copy-start(bf16[1280,64]{0,1:T(8,128)(2,1)} %get-tuple-element.369) | copy-start | bytes 491524 | tf_op jit(solution)/shard_map/while
  377.3 3.6 copy-start.2
  510.2 31.5 %copy-start.1 = (bf16[1024,8,128]{0,2,1:T(8,128)(2,1)S(1)}, bf16[1024,8,128]{0,2,1:T(8,128)(2,1)}, u32[]{:S(2)}) copy-start(bf16[1024,8,128]{0,2,1:T(8,128)(2,1)} %get-tuple-element.337) | copy-start | bytes 6291460 | tf_op jit(solution)/shard_map/while
  558.8 35.2 %copy-start.5 = (bf16[1280,64]{0,1:T(8,128)(2,1)S(1)}, bf16[1280,64]{0,1:T(8,128)(2,1)}, u32[]{:S(2)}) copy-start(bf16[1280,64]{0,1:T(8,128)(2,1)} %get-tuple-element.369) | copy-start | bytes 491524 | tf_op jit(solution)/shard_map/while
  599.7 4.5 slice-start
  602.6 1.6 slice-start.1
  604.2 1.2 copy-start.10
  607.0 10.7 %collective-permute-start.3 = (f32[256,576]{0,1:T(8,128)S(1)}, f32[256,576]{0,1:T(8,128)S(1)}, u32[]{:S(2)}, u32[]{:S(2)}) collective-permute-start(f32[256,576]{0,1:T(8,128)S(1)} %pad_maximum_fusion.2), channel_id=1, source_target_pairs={{1,0},{2,1},{3,2},{4,3},{5,4},{6,5},{7,6},{8,7},{9,8},{10,9},{11,1... | collective-permute-start | bytes 1769480 | tf_op jit(solution)/shard_map/ppermute | solution.py:22
Sparse Core Ops, SparseCore 0:
  11.8 59.7 all-gather.1
  619.6 59.7 reduce-scatter.1
where the time goes:
time: 697 us; the launch traced here: 689 us
  matrix products  359 us (52%)
  local copies, waits for them, and re-layouts  122 us (18%)
  waiting for transfers between devices  91.6 us (13%)
  other arithmetic  56.3 us (8%)
  loops' own time  27 us (4%)
  starting transfers between devices  18.2 us (3%)
  between operations  14.5 us (2%)
    dot_general x2, matrix products, attend_block(): jnp.einsum('hrk,khd->rhd', grad_scores, span_keys, preferred_element_type...  82.6 us
    dot_general x2, matrix products, attend_block(): jnp.einsum('hrk,rhd->khd', grad_scores, block_nope, preferred_element_typ...  70.3 us
    dot_general x2, matrix products, attend_block(): jnp.einsum('hrk,kd->rhd', grad_scores, span_rot, preferred_element_type=j...  64.6 us
    dot_general x2, matrix products, attend_block(): jnp.einsum('hrk,rhd->kd', grad_scores, block_rot, preferred_element_type=...  62.9 us
    dynamic_update_slice x8, local copies, waits for them, and re-layouts, per_device(): lax.scan(attend_block, initial, jnp.arange(group_tok // row_count, dtype=...  51.4 us
    all_gather x1, waiting for transfers between devices, per_device(): rows_piece = lax.all_gather(own_piece, 'grp', axis=0, tiled=True)  48.9 us
    dot_general x2, matrix products, attend_block(): jnp.einsum('hrk,rhd->khd', attention_low, block_grad, preferred_element_t...  34.4 us
    reduce_scatter x1, waiting for transfers between devices, per_device(): lax.psum_scatter(own_part + jnp.concatenate([leading, returned], axis=0),...  32.6 us
  transfers between devices with their start and end apart: 7, of which 4 were waited for; matrix products, arithmetic and copies ran while one was open for 8% of the time, Pallas kernels for 0%

commit v1 on v0

v1 whole, which is shorter than its diff:
```python
import math

import jax
import jax.numpy as jnp
import numpy as np
from jax import lax
from jax.experimental import pallas as pl
from jax.experimental.pallas import tpu as pltpu
from jax.sharding import PartitionSpec as P

D_C = 512
D_R = 64
D_N = 128
D_V = 128
LANES = 128
BIG = -1e30

rope_base = 10000.0
yarn_factor = 40.0
pretrain_context = 4096.0

mscale = 0.1 * math.log(yarn_factor) + 1.0
SCALING = (D_N + D_R) ** (-0.5) * mscale * mscale

F32 = jnp.float32
BF16 = jnp.bfloat16
NT = (((1,), (1,)), ((), ()))
TN = (((0,), (0,)), ((), ()))
NN = (((1,), (0,)), ((), ()))


def dot(a, b, dims):
    return lax.dot_general(a, b, dims, preferred_element_type=F32)


def freqs_of(width):
    half_width = width // 2
    index = np.arange(half_width, dtype=np.float64)
    extrapolated = rope_base ** (-2.0 * index / width)
    span = 2.0 * math.log(rope_base)
    lowest = max(math.floor(width * math.log(pretrain_context / (64.0 * math.pi)) / span), 0)
    highest = min(math.ceil(width * math.log(pretrain_context / (2.0 * math.pi)) / span), width - 1)
    ramp = np.clip((index - lowest) / (highest - lowest), 0.0, 1.0)
    return (extrapolated / yarn_factor * ramp + extrapolated * (1.0 - ramp)).astype(np.float32)


def lane_of(rows):
    return lax.broadcasted_iota(jnp.int32, (rows, LANES), 1)


def swap_halves(m):
    lane = lane_of(m.shape[0])
    return jnp.where((lane & 32) == 0, pltpu.roll(m, 96, 1), pltpu.roll(m, 32, 1))


def from_behind(block, axis, distance):
    n = lax.axis_size(axis)
    route = [(i - distance, i) for i in range(n) if 0 <= i - distance < n]
    return lax.ppermute(block, axis, route)


def project_rows(first, rows, lat, key_up, value_up, kslot, krot, values):
    span = pl.ds(first, rows)
    low = lane_of(rows) < 64
    compressed = lat[span, :D_C]
    both = lat[span, D_C:].astype(F32)
    krot[span, :] = jnp.where(low, both, 0.0).astype(BF16)

    def pair(p, _):
        source = pl.ds(pl.multiple_of(p * 256, 256), 256)
        keys = dot(compressed, key_up[:, source], NN)
        values[span, source] = dot(compressed, value_up[:, source], NN).astype(BF16)
        turned = pltpu.roll(keys[:, 128:], 64, 1)
        kslot[span, pl.ds(pl.multiple_of(p * 384, 128), 128)] = keys[:, :128].astype(BF16)
        kslot[span, pl.ds(pl.multiple_of(p * 384 + 128, 128), 128)] = jnp.where(low, 0.0, turned).astype(BF16)
        kslot[span, pl.ds(pl.multiple_of(p * 384 + 256, 128), 128)] = jnp.where(low, turned, both).astype(BF16)
        return 0

    lax.fori_loop(0, key_up.shape[1] // 256, pair, 0)


def turn_queries(first, rows, qbuf, cos, sin):
    span = pl.ds(first, rows)
    low = lane_of(rows) < 64
    c, s = cos[span, :], sin[span, :]

    def pair(p, _):
        at1 = pl.ds(pl.multiple_of(p * 384 + 128, 128), 128)
        at2 = pl.ds(pl.multiple_of(p * 384 + 256, 128), 128)
        one, two = qbuf[span, at1].astype(F32), qbuf[span, at2].astype(F32)
        m = jnp.where(low, one, two)
        r = m * c + swap_halves(m) * s
        qbuf[span, at1] = jnp.where(low, r, one).astype(BF16)
        qbuf[span, at2] = jnp.where(low, two, r).astype(BF16)
        return 0

    lax.fori_loop(0, qbuf.shape[1] // 384, pair, 0)


def fill_bias(first, pos, bias):
    for half in range(2):
        p = pos[0:1, pl.ds(pl.multiple_of(first + half * 128, 128), 128)]
        c = lax.broadcasted_iota(jnp.int32, (384, 128), 0)
        r = lax.broadcasted_iota(jnp.int32, (384, 128), 1) + 256
        seen = (c <= r) & (c >= r - p)
        bias[half] = jnp.where(seen, 0.0, BIG)


def weigh(scores, dprob, bias):
    probs, grads = [], []
    for half in range(2):
        rows, cols = slice(128 * half, 128 * half + 384), slice(128 * half, 128 * half + 128)
        s = scores[rows, cols] + bias[half]
        d = dprob[rows, cols]
        top = jnp.max(s, axis=0, keepdims=True)
        e = jnp.exp((s - top) * SCALING)
        total = jnp.sum(e, axis=0, keepdims=True)
        delta = jnp.sum(e * d, axis=0, keepdims=True) / total
        prob = e * (1.0 / total)
        grad = (prob * (d - delta) * SCALING).astype(BF16)
        prob = prob.astype(BF16)
        none = jnp.zeros((128, 128), BF16)
        order = (lambda x: [x, none]) if half == 0 else (lambda x: [none, x])
        probs.append(jnp.concatenate(order(prob), axis=0))
        grads.append(jnp.concatenate(order(grad), axis=0))
    return jnp.concatenate(probs, axis=1), jnp.concatenate(grads, axis=1)


def attend(first, qbuf, gout, kslot, krot, values, bias, cos, sin, dq, dkacc, dvacc):
    qs, ks = pl.ds(first, 256), pl.ds(first, 512)

    def pair(p, _):
        s0 = pl.multiple_of(p * 384, 128)
        v0 = pl.multiple_of(p * 256, 256)
        q = qbuf[qs, pl.ds(s0, 384)]
        g = gout[qs, pl.ds(v0, 256)]
        k0 = jnp.concatenate([kslot[ks, pl.ds(s0, 128)], krot[ks, :]], axis=1)
        k1 = kslot[ks, pl.ds(pl.multiple_of(s0 + 128, 128), 256)]
        dqs, dks = [], []
        for odd, k in ((0, k0), (1, k1)):
            qh = q[:, 128 * odd : 128 * odd + 256]
            gh = g[:, 128 * odd : 128 * odd + 128]
            vh = values[ks, pl.ds(pl.multiple_of(v0 + 128 * odd, 128), 128)]
            scores = dot(k, qh, NT)
            dprob = dot(vh, gh, NT)
            prob, grad = weigh(scores, dprob, bias)
            dvacc[ks, pl.ds(pl.multiple_of(v0 + 128 * odd, 128), 128)] += dot(prob, gh, NN)
            dks.append(dot(grad, qh, NN))
            dqs.append(dot(grad, k, TN))
        low = lane_of(512) < 64
        dkacc[ks, pl.ds(s0, 128)] += dks[0][:, :128]
        dkacc[ks, pl.ds(pl.multiple_of(s0 + 128, 128), 128)] += jnp.where(low, dks[0][:, 128:], dks[1][:, :128])
        dkacc[ks, pl.ds(pl.multiple_of(s0 + 256, 128), 128)] += dks[1][:, 128:]
        low = lane_of(256) < 64
        one, two = dqs[0][:, 128:] + dqs[1][:, :128], dqs[1][:, 128:]
        m = jnp.where(low, one, two)
        r = m * cos[qs, :] - swap_halves(m) * sin[qs, :]
        dq[qs, pl.ds(s0, 128)] = dqs[0][:, :128].astype(BF16)
        dq[qs, pl.ds(pl.multiple_of(s0 + 128, 128), 128)] = jnp.where(low, r, one).astype(BF16)
        dq[qs, pl.ds(pl.multiple_of(s0 + 256, 128), 128)] = jnp.where(low, two, r).astype(BF16)
        return 0

    lax.fori_loop(0, qbuf.shape[1] // 384, pair, 0)


def gather_back(first, rows, key_up, value_up, dkacc, dvacc):
    span = pl.ds(first, rows)
    low = lane_of(rows) < 64
    total = jnp.zeros((rows, D_C), F32)
    turn = jnp.zeros((rows, LANES), F32)
    for p in range(key_up.shape[1] // 256):
        one = dkacc[span, 384 * p + 128 : 384 * p + 256]
        two = dkacc[span, 384 * p + 256 : 384 * p + 384]
        turn = turn + jnp.where(low, one, two)
        odd = pltpu.roll(jnp.where(low, two, one), 64, 1).astype(BF16)
        even = dkacc[span, 384 * p : 384 * p + 128].astype(BF16)
        cols = slice(256 * p, 256 * p + 256)
        total = total + dot(jnp.concatenate([even, odd], axis=1), key_up[:, cols], NT)
        total = total + dot(dvacc[span, cols].astype(BF16), value_up[:, cols], NT)
    return total, turn + pltpu.roll(turn, 64, 1)


def kernel(pos, qin, gout, lat, key_up, value_up, cos, sin, dq, part, qbuf, kslot, krot, values, bias, dkacc, dvacc):
    group_tok = qin.shape[0]
    qbuf[...] = qin[...]
    dkacc[...] = jnp.zeros_like(dkacc)
    dvacc[...] = jnp.zeros_like(dvacc)

    def prepare(j, _):
        project_rows(pl.multiple_of(j * 256, 256), 256, lat, key_up, value_up, kslot, krot, values)
        return 0

    lax.fori_loop(0, group_tok // 256 + 1, prepare, 0)

    def block(t, _):
        first = pl.multiple_of(t * 256, 256)
        turn_queries(first, 256, qbuf, cos, sin)
        fill_bias(first, pos, bias)
        attend(first, qbuf, gout, kslot, krot, values, bias, cos, sin, dq, dkacc, dvacc)
        return 0

    lax.fori_loop(0, group_tok // 256, block, 0)

    def finish(j, _):
        first = pl.multiple_of(j * 256, 256)
        total, turn = gather_back(first, 256, key_up, value_up, dkacc, dvacc)
        part[pl.ds(first, 256), :D_C] = total
        part[pl.ds(first, 256), D_C:] = turn
        return 0

    lax.fori_loop(0, group_tok // 256 + 1, finish, 0)


def per_device(query, latent, positions, key_up, value_up, grad_out):
    tok_dev = query.shape[1]
    group_tok = tok_dev * lax.axis_size("grp")
    key_rows = 256 + group_tok
    slots = query.shape[2] // lax.axis_size("grp")
    width = key_up.shape[1]
    freq = jnp.asarray(np.tile(freqs_of(D_R), 4))
    sign = jnp.asarray(np.where(np.arange(LANES) % 64 < 32, -1.0, 1.0).astype(np.float32))
    angles = positions[0].astype(F32)[:, None] * freq[None, :]
    cos, sin = jnp.cos(angles), jnp.sin(angles) * sign[None, :]
    own = lax.axis_index("grp") * tok_dev
    own_cos = lax.dynamic_slice_in_dim(cos, own, tok_dev, 0)[:, :D_R]
    own_sin = lax.dynamic_slice_in_dim(sin, own, tok_dev, 0)[:, :D_R]

    def turned(u, way):
        return u * own_cos + way * jnp.concatenate([u[:, 32:], u[:, :32]], axis=1) * own_sin

    rot = turned(latent[0, :, D_C:].astype(F32), 1.0).astype(BF16)
    piece = jnp.concatenate([latent[0, :, :D_C], rot, rot], axis=1)
    rows = lax.all_gather(piece, "grp", axis=0, tiled=True)
    query_heads = lax.all_to_all(query[0], "grp", split_axis=1, concat_axis=0, tiled=True)
    lat = jnp.concatenate([from_behind(rows[group_tok - 256 :], "blk", 1), rows], axis=0)
    grad_query, part = pl.pallas_call(
        kernel,
        out_shape=(
            jax.ShapeDtypeStruct((group_tok, slots), BF16),
            jax.ShapeDtypeStruct((key_rows, D_C + LANES), F32),
        ),
        in_specs=[pl.BlockSpec(memory_space=pltpu.VMEM)] * 8,
        out_specs=(pl.BlockSpec(memory_space=pltpu.VMEM),) * 2,
        scratch_shapes=[
            pltpu.VMEM((group_tok, slots), BF16),
            pltpu.VMEM((key_rows, slots), BF16),
            pltpu.VMEM((key_rows, LANES), BF16),
            pltpu.VMEM((key_rows, width), BF16),
            pltpu.VMEM((2, 384, 128), F32),
            pltpu.VMEM((key_rows, slots), F32),
            pltpu.VMEM((key_rows, width), F32),
        ],
        compiler_params=pltpu.CompilerParams(vmem_limit_bytes=60 * 1024 * 1024),
    )(positions, query_heads, grad_out[0], lat, key_up, value_up, cos, sin)
    part = part[:, : D_C + D_R]
    own_part = part[256:]
    returned = from_behind(part[:256], "blk", -1)
    own_part = jnp.concatenate([own_part[: group_tok - 256], own_part[group_tok - 256 :] + returned], axis=0)
    summed = lax.psum_scatter(own_part, "grp", scatter_dimension=0, tiled=True)
    grad_latent = jnp.concatenate([summed[:, :D_C], turned(summed[:, D_C:], -1.0)], axis=1).astype(BF16)
    return (grad_query[None], grad_latent[None])


def solution(mesh):
    placed = (
        P("blk", "grp", None),
        P("blk", "grp", None),
        P("blk", None),
        P(None, "grp"),
        P(None, "grp"),
        P("blk", None, "grp"),
    )
    return jax.shard_map(
        per_device,
        mesh=mesh,
        in_specs=placed,
        out_specs=(P("blk", None, "grp"), P("blk", "grp", None)),
        check_vma=False,
    )
```

time: 697 us -> 228 us (0.33)
  matrix products: 359 us -> 0 us
  local copies, waits for them, and re-layouts: 122 us -> 17.2 us
  other arithmetic: 56.3 us -> 10.6 us
  Pallas kernels: 0 us -> 44.2 us
  waiting for transfers between devices: 91.6 us -> 128 us
  loops' own time: 27 us -> 0 us
    dot_general x20 -> x0, matrix products: 359 us -> none  [the longest x2 82.6 us: attend_block(): jnp.einsum('hrk,khd->rhd', grad_scores, span_keys, preferred_element_type...]
    dynamic_update_slice x8 -> x0, local copies, waits for them, and re-layouts: 51.4 us -> none  [per_device(): lax.scan(attend_block, initial, jnp.arange(group_tok // row_count, dtype=...]
    pallas_call x0 -> x1, Pallas kernels: none -> 44.2 us  [per_device(): pl.pallas_call(kernel, out_shape=(jax.ShapeDtypeStruct((group_tok, slots)...]
    sub x4 -> x0, other arithmetic: 30.3 us -> none  [the longest x2 30.2 us: attend_block(): weights = jnp.exp(scores - top_score)]
    reduce_scatter x1, waiting for transfers between devices: 32.6 us -> 62.4 us  [per_device(): summed = lax.psum_scatter(own_part, 'grp', scatter_dimension=0, tiled=True)]
    another operation x1 -> x0, loops' own time: 27 us -> none  [per_device(): lax.scan(attend_block, initial, jnp.arange(group_tok // row_count, dtype=...]
    unnamed x25 -> x10, local copies, waits for them, and re-layouts: 18.5 us -> 6.69 us
    another operation x4 -> x0, local copies, waits for them, and re-layouts: 11.3 us -> none
  transfers between devices with their start and end apart: 7 -> 5, of which waited for: 4 -> 4; matrix products, arithmetic and copies ran while one was open for 8% -> 5% of each run, Pallas kernels for 0% -> 0%
where the time goes in v1:
time: 228 us; the launch traced here: 226 us
  waiting for transfers between devices  128 us (56%)
  Pallas kernels  44.2 us (19%)
  local copies, waits for them, and re-layouts  17.2 us (8%)
  between operations  14.2 us (6%)
  starting transfers between devices  11.7 us (5%)
  other arithmetic  10.6 us (5%)
    reduce_scatter x1, waiting for transfers between devices, per_device(): summed = lax.psum_scatter(own_part, 'grp', scatter_dimension=0, tiled=True)  62.4 us
    all_gather x1, waiting for transfers between devices, per_device(): rows = lax.all_gather(piece, 'grp', axis=0, tiled=True)  51.3 us
    pallas_call x1, Pallas kernels, per_device(): pl.pallas_call(kernel, out_shape=(jax.ShapeDtypeStruct((group_tok, slots)...  44.2 us
    ppermute x2, waiting for transfers between devices, from_behind(): return lax.ppermute(block, axis, route)  14.7 us
    unnamed x10, local copies, waits for them, and re-layouts  6.69 us
    all_to_all x1, starting transfers between devices, per_device(): lax.all_to_all(query[0], 'grp', split_axis=1, concat_axis=0, tiled=True)  6.33 us
    ppermute x2, starting transfers between devices, from_behind(): return lax.ppermute(block, axis, route)  5.28 us
  transfers between devices with their start and end apart: 5, of which 4 were waited for; matrix products, arithmetic and copies ran while one was open for 5% of the time, Pallas kernels for 0%

profile of v1, /device:TPU:6, one launch (start us, length us, event | category | flops | bytes accessed | tf_op | source)
XLA Modules:
  0.0 226.3 jit_solution(1527119278144106912)
XLA Ops:
  7.2 0.7 slice.52
  7.9 0.9 slice.51
  8.9 0.7 convert_element_type.29
  9.5 0.1 copy.21
  9.8 0.1 copy.20
  9.9 2.6 %multiply_cosine_fusion = (f32[1024,128]{1,0:T(8,128)S(1)}, f32[1024,128]{1,0:T(8,128)S(1)}) fusion(f32[128]{0:T(128)} %constant.18.clone, f32[1024]{0:T(1024)S(1)} %bitcast.24, f32[128]{0:T(128)} %constant.19.clone), kind=kLoop, calls=%fused_computation.3 | loop fusion | flops 262144 | bytes 1053696 | tf_op jit(solution)/shard_map/cos | solution.py:223
  12.5 0.8 copy-done.1
  13.3 0.1 fusion.5
  13.5 0.7 pad_maximum_fusion.2
  14.3 3.1 %copy.22 = bf16[16,8,8,1536]{3,2,1,0:T(8,128)(2,1)S(1)} copy(bf16[16,8,8,1536]{3,1,2,0:T(8,128)(2,1)} %bitcast.21) | data formatting | bytes 6291456
  17.3 2.6 %copy.14 = bf16[128,8,1536]{2,0,1:T(8,128)(2,1)} copy(bf16[128,8,1536]{2,1,0:T(8,128)(2,1)S(1)} %bitcast.19) | data formatting | bytes 6291456 | tf_op jit(solution)/shard_map/all_to_all | solution.py:234
  19.9 6.3 %all-to-all-start = ((bf16[128,8,1536]{2,0,1:T(8,128)(2,1)}), bf16[128,8,1536]{2,0,1:T(8,128)(2,1)S(1)}, u32[]{:S(2)}, u32[]{:S(2)}) async-start(bf16[128,8,1536]{2,0,1:T(8,128)(2,1)} %copy.14), calls=%async_computation | async-start | bytes 6291456 | tf_op jit(solution)/shard_map/all_to_all | solution.py:234
  26.3 51.3 %all-gather.2.cloned.1.call-done = bf16[1024,640]{1,0:T(8,128)(2,1)} async-done(((bf16[128,640]{1,0:T(8,128)(2,1)}), bf16[1024,640]{1,0:T(8,128)(2,1)}) %all-gather.2.cloned.1.call-update) | async-done | bytes 1310736 | tf_op jit(solution)/shard_map/all_gather | solution.py:233
  77.6 1.0 slice.67
  78.6 1.9 collective-permute-start
  80.5 9.0 %collective-permute-done = bf16[256,640]{1,0:T(8,128)(2,1)S(1)} collective-permute-done((bf16[256,640]{1,0:T(8,128)(2,1)S(1)}, bf16[256,640]{1,0:T(8,128)(2,1)S(1)}, u32[]{:S(2)}, u32[]{:S(2)}) %collective-permute-start) | collective-permute-done | bytes 327712 | tf_op jit(solution)/shard_map/ppermute | solution.py:59
  89.5 2.6 %pad_maximum_fusion.1.lat = bf16[1280,640]{1,0:T(8,128)(2,1)} fusion(bf16[1024,640]{1,0:T(8,128)(2,1)} %all-gather.2.cloned.1.call-done, bf16[256,640]{1,0:T(8,128)(2,1)S(1)} %collective-permute-done), kind=kLoop, calls=%fused_computation.1 | loop fusion | flops 3276800 | bytes 3276800 | tf_op jit(solution)/shard_map/concatenate | solution.py:235
  92.1 1.7 copy-done
  93.8 44.2 %shard_map.95 = (bf16[1024,1536]{1,0:T(8,128)(2,1)}, f32[1280,640]{1,0:T(8,128)}) custom-call(s32[1,1024]{1,0:T(1,128)} %pos.1, bf16[1024,1536]{1,0:T(8,128)(2,1)} %bitcast.20, bf16[1024,1024]{1,0:T(8,128)(2,1)} %bitcast.22, bf16[1280,640]{1,0:T(8,128)(2,1)} %pad_maximum_fusion.1.lat, bf16[512,1024]{1,0:T(8,128)(2,1)} %key_up.1, bf16[512,1024]{1,0:T(8,128)(2,1)} %value_up.1, ...), custom_call_target="tpu_custom_call" | custom-call | tf_op jit(solution)/shard_map/pallas_call | solution.py:236
  138.0 1.1 slice.60
  139.2 0.2 copy.17
  139.4 3.4 %collective-permute-start.1 = (f32[256,576]{0,1:T(8,128)S(1)}, f32[256,576]{0,1:T(8,128)S(1)}, u32[]{:S(2)}, u32[]{:S(2)}) collective-permute-start(f32[256,576]{0,1:T(8,128)S(1)} %copy.17), channel_id=1, source_target_pairs={{1,0},{2,1},{3,2},{4,3},{5,4},{6,5},{7,6},{8,7},{9,8},{10,9},{11,1... | collective-permute-start | bytes 1769480 | tf_op jit(solution)/shard_map/ppermute | solution.py:59
  142.7 1.7 slice.58
  144.4 5.7 %collective-permute-done.1 = f32[256,576]{0,1:T(8,128)S(1)} collective-permute-done((f32[256,576]{0,1:T(8,128)S(1)}, f32[256,576]{0,1:T(8,128)S(1)}, u32[]{:S(2)}, u32[]{:S(2)}) %collective-permute-start.1) | collective-permute-done | bytes 589856 | tf_op jit(solution)/shard_map/ppermute | solution.py:59
  150.1 0.2 copy.18
  150.4 1.2 slice_add_fusion
  151.5 1.7 pad_maximum_fusion
  153.2 62.4 %reduce-scatter.2.cloned.1.call-done = f32[128,576]{1,0:T(8,128)} async-done(((f32[1024,576]{1,0:T(8,128)}), f32[128,576]{1,0:T(8,128)}) %reduce-scatter.2.cloned.1.call-update) | async-done | bytes 294928 | tf_op jit(solution)/shard_map/reduce_scatter | solution.py:259
  215.7 1.0 fusion.1
  216.6 1.0 fusion.8
  217.6 1.0 fusion.7
  218.7 0.8 copy.19
  (12 shorter events, 0.3 us)
Async XLA Ops:
  7.2 70.4 %all-gather.2.cloned.1.call-start = ((), (), s32[]{:S(2)}) async-start(), calls=%async_computation.2 | async-start | bytes 1474560 | tf_op jit(solution)/shard_map/all_gather | solution.py:233
  12.5 0.9 copy-start.1
  12.5 1.0 copy-start.2
  19.9 72.2 %all-to-all-start = ((bf16[128,8,1536]{2,0,1:T(8,128)(2,1)}), bf16[128,8,1536]{2,0,1:T(8,128)(2,1)S(1)}, u32[]{:S(2)}, u32[]{:S(2)}) async-start(bf16[128,8,1536]{2,0,1:T(8,128)(2,1)} %copy.14), calls=%async_computation | async-start | bytes 6291456 | tf_op jit(solution)/shard_map/all_to_all | solution.py:234
  26.3 189.4 %reduce-scatter.2.cloned.1.call-start = ((), (), s32[]{:S(2)}) async-start(), calls=%async_computation.3 | async-start | bytes 2949120 | tf_op jit(solution)/shard_map/reduce_scatter | solution.py:259
  78.6 10.9 %collective-permute-start = (bf16[256,640]{1,0:T(8,128)(2,1)S(1)}, bf16[256,640]{1,0:T(8,128)(2,1)S(1)}, u32[]{:S(2)}, u32[]{:S(2)}) collective-permute-start(bf16[256,640]{1,0:T(8,128)(2,1)S(1)} %slice.67), channel_id=1, source_target_pairs={{0,1},{1,2},{2,3},{3,4},{4,5},{5,6},{6,7},{7,8},{8,9},{9,10},{10,1... | collective-permute-start | bytes 983048 | tf_op jit(solution)/shard_map/ppermute | solution.py:59
  92.1 1.7 copy-start
  139.4 10.7 %collective-permute-start.1 = (f32[256,576]{0,1:T(8,128)S(1)}, f32[256,576]{0,1:T(8,128)S(1)}, u32[]{:S(2)}, u32[]{:S(2)}) collective-permute-start(f32[256,576]{0,1:T(8,128)S(1)} %copy.17), channel_id=1, source_target_pairs={{1,0},{2,1},{3,2},{4,3},{5,4},{6,5},{7,6},{8,7},{9,8},{10,9},{11,1... | collective-permute-start | bytes 1769480 | tf_op jit(solution)/shard_map/ppermute | solution.py:59
Sparse Core Ops, SparseCore 0:
  14.4 63.1 all-gather.1
  153.3 62.2 reduce-scatter.1

commit v2 on v1

--- a/solution.py
+++ b/solution.py
@@ -53,10 +53,13 @@
     return jnp.where((lane & 32) == 0, pltpu.roll(m, 96, 1), pltpu.roll(m, 32, 1))
 
 
-def from_behind(block, axis, distance):
-    n = lax.axis_size(axis)
-    route = [(i - distance, i) for i in range(n) if 0 <= i - distance < n]
-    return lax.ppermute(block, axis, route)
+def fill_tables(first, pos, freq, cos, sin):
+    p = pos[0:1, pl.ds(pl.multiple_of(first, 128), 128)].astype(F32)
+    angles = jnp.broadcast_to(p, (128, 128)).T * freq[0:1, :]
+    span = pl.ds(first, 128)
+    cos[span, :] = jnp.cos(angles)
+    s = jnp.sin(angles)
+    sin[span, :] = jnp.where((lane_of(128) & 32) == 0, -s, s)
 
 
 def project_rows(first, rows, lat, key_up, value_up, kslot, krot, values):
@@ -180,35 +183,166 @@
     return total, turn + pltpu.roll(turn, 64, 1)
 
 
-def kernel(pos, qin, gout, lat, key_up, value_up, cos, sin, dq, part, qbuf, kslot, krot, values, bias, dkacc, dvacc):
-    group_tok = qin.shape[0]
-    qbuf[...] = qin[...]
+STEPS = ((0, 1), (1, 0), (1, 1), (3, 0), (3, 1), (2, 0), (2, 1))
+
+
+def kernel(
+    query, gout_hbm, lat_in, pos, key_hbm, value_hbm, freq, dq_hbm, glat,
+    qbuf, lat, gout, key_up, value_up, cos, sin, kslot, krot, values, bias, dkacc, dvacc, dq, sbuf, own, rbuf, hbuf,
+    load_sem, store_sem, lat_send, lat_recv, q_send, q_recv, g_send, g_recv, h_send, h_recv,
+):
+    g, b = lax.axis_index("grp"), lax.axis_index("blk")
+    nb = lax.axis_size("blk")
+    z, y = g // 2, g % 2
+    slots = qbuf.shape[1]
+    group_tok = qbuf.shape[0]
+    ahead, behind = (b + 1) % nb, (b + nb - 1) % nb
+
+    def peer(step, way=1):
+        return ((z + 4 + way * step[0]) % 4) * 2 + (y + step[1]) % 2
+
+    def remote(src, dst, send, recv, to_g=None, to_b=None):
+        return pltpu.make_async_remote_copy(
+            src_ref=src,
+            dst_ref=dst,
+            send_sem=send,
+            recv_sem=recv,
+            device_id=(g if to_g is None else to_g, b if to_b is None else to_b),
+            device_id_type=pl.DeviceIdType.MESH,
+        )
+
+    loads = [
+        pltpu.make_async_copy(key_hbm, key_up, load_sem.at[0]),
+        pltpu.make_async_copy(value_hbm, value_up, load_sem.at[1]),
+        pltpu.make_async_copy(
+            query.at[:, pl.ds(pl.multiple_of(g * slots, 128), slots)],
+            qbuf.at[pl.ds(pl.multiple_of(g * 128, 128), 128), :],
+            load_sem.at[2],
+        ),
+        pltpu.make_async_copy(gout_hbm, gout, load_sem.at[3]),
+    ]
+    for load in loads:
+        load.start()
+
+    barrier = pltpu.get_barrier_semaphore()
+    for step in STEPS:
+        pl.semaphore_signal(barrier, inc=1, device_id=(peer(step), b), device_id_type=pl.DeviceIdType.MESH)
+    for other in (ahead, behind):
+        pl.semaphore_signal(barrier, inc=1, device_id=(g, other), device_id_type=pl.DeviceIdType.MESH)
+
+    my = pl.multiple_of(g * 128, 128)
+    mine = pl.ds(my, 128)
+    fill_tables(my, pos, freq, cos, sin)
+    raw = lat_in[:, D_C:].astype(F32)
+    raw = jnp.concatenate([raw, raw], axis=1)
+    turned = (raw * cos[mine, :] + swap_halves(raw) * sin[mine, :]).astype(BF16)
+    my_rows = pl.ds(pl.multiple_of(256 + g * 128, 128), 128)
+    lat[my_rows, :D_C] = lat_in[:, :D_C]
+    lat[my_rows, D_C:] = turned
+
+    pl.semaphore_wait(barrier, 9)
+    lat_copies = [
+        remote(lat.at[my_rows, :], lat.at[my_rows, :], lat_send.at[i], lat_recv.at[i], to_g=peer(step))
+        for i, step in enumerate(STEPS)
+    ]
+    for copy in lat_copies:
+        copy.start()
+    q_copies = [
+        remote(
+            query.at[:, pl.ds(pl.multiple_of(peer(step) * slots, 128), slots)],
+            qbuf.at[mine, :],
+            q_send.at[i],
+            q_recv.at[i],
+            to_g=peer(step),
+        )
+        for i, step in enumerate(STEPS)
+    ]
+    for copy in q_copies:
+        copy.start()
+
     dkacc[...] = jnp.zeros_like(dkacc)
     dvacc[...] = jnp.zeros_like(dvacc)
+
+    def table(t, _):
+        fill_tables(pl.multiple_of(t * 128, 128), pos, freq, cos, sin)
+        return 0
+
+    lax.fori_loop(0, group_tok // 128, table, 0)
+
+    for copy in lat_copies:
+        copy.wait_recv()
+    halo = remote(lat.at[pl.ds(group_tok, 256), :], lat.at[pl.ds(0, 256), :], h_send.at[0], h_recv.at[0], to_b=ahead)
+    halo.start()
+    loads[0].wait()
+    loads[1].wait()
 
     def prepare(j, _):
         project_rows(pl.multiple_of(j * 256, 256), 256, lat, key_up, value_up, kslot, krot, values)
         return 0
 
-    lax.fori_loop(0, group_tok // 256 + 1, prepare, 0)
-
-    def block(t, _):
-        first = pl.multiple_of(t * 256, 256)
+    lax.fori_loop(1, group_tok // 256 + 1, prepare, 0)
+    halo.wait_recv()
+    prepare(0, 0)
+    loads[2].wait()
+    loads[3].wait()
+
+    stores = []
+    for i, (way, arrivals) in enumerate(((0, (0,)), (-1, (1, 2)), (1, (3, 4)), (2, (5, 6)))):
+        for a in arrivals:
+            q_copies[a].wait_recv()
+        first = pl.multiple_of(((z + 4 + way) % 4) * 256, 256)
         turn_queries(first, 256, qbuf, cos, sin)
         fill_bias(first, pos, bias)
         attend(first, qbuf, gout, kslot, krot, values, bias, cos, sin, dq, dkacc, dvacc)
-        return 0
-
-    lax.fori_loop(0, group_tok // 256, block, 0)
-
-    def finish(j, _):
-        first = pl.multiple_of(j * 256, 256)
+        store = pltpu.make_async_copy(dq.at[pl.ds(first, 256), :], dq_hbm.at[pl.ds(first, 256), :], store_sem.at[i])
+        store.start()
+        stores.append(store)
+
+    total, turn = gather_back(0, 256, key_up, value_up, dkacc, dvacc)
+    sbuf[0:256, :D_C] = total.astype(BF16)
+    sbuf[0:256, D_C:] = turn.astype(BF16)
+    back = remote(sbuf.at[0:256, :], hbuf, h_send.at[1], h_recv.at[1], to_b=behind)
+    back.start()
+
+    g_copies = []
+    for way in (2, 1, 3, 0):
+        block = (z + way) % 4
+        first = pl.multiple_of(256 + block * 256, 256)
         total, turn = gather_back(first, 256, key_up, value_up, dkacc, dvacc)
-        part[pl.ds(first, 256), :D_C] = total
-        part[pl.ds(first, 256), D_C:] = turn
-        return 0
-
-    lax.fori_loop(0, group_tok // 256 + 1, finish, 0)
+        own[:, :D_C] = total
+        own[:, D_C:] = turn
+
+        @pl.when(block == 3)
+        def _():
+            back.wait_recv()
+            own[...] += hbuf[...].astype(F32)
+
+        if way:
+            sbuf[pl.ds(first, 256), :] = own[...].astype(BF16)
+        else:
+            first = pl.multiple_of(first + (1 - y) * 128, 128)
+            sbuf[pl.ds(first, 128), :] = own[pl.ds(pl.multiple_of((1 - y) * 128, 128), 128), :].astype(BF16)
+        for i, step in enumerate(STEPS):
+            if step[0] == way:
+                rows = pl.ds(pl.multiple_of(256 + peer(step) * 128, 128), 128)
+                copy = remote(sbuf.at[rows, :], rbuf.at[i], g_send.at[i], g_recv.at[i], to_g=peer(step))
+                copy.start()
+                g_copies.append(copy)
+
+    total = own[pl.ds(pl.multiple_of(y * 128, 128), 128), :]
+    for copy in g_copies:
+        copy.wait_recv()
+    for i in range(len(STEPS)):
+        total = total + rbuf[i].astype(F32)
+    turn = total[:, D_C:]
+    turn = turn * cos[mine, :] - swap_halves(turn) * sin[mine, :]
+    glat[:, :D_C] = total[:, :D_C].astype(BF16)
+    glat[:, D_C:] = turn[:, :D_R].astype(BF16)
+
+    for copy in lat_copies + q_copies + g_copies + [halo, back]:
+        copy.wait_send()
+    for store in stores:
+        store.wait()
 
 
 def per_device(query, latent, positions, key_up, value_up, grad_out):
@@ -217,47 +351,52 @@
     key_rows = 256 + group_tok
     slots = query.shape[2] // lax.axis_size("grp")
     width = key_up.shape[1]
-    freq = jnp.asarray(np.tile(freqs_of(D_R), 4))
-    sign = jnp.asarray(np.where(np.arange(LANES) % 64 < 32, -1.0, 1.0).astype(np.float32))
-    angles = positions[0].astype(F32)[:, None] * freq[None, :]
-    cos, sin = jnp.cos(angles), jnp.sin(angles) * sign[None, :]
-    own = lax.axis_index("grp") * tok_dev
-    own_cos = lax.dynamic_slice_in_dim(cos, own, tok_dev, 0)[:, :D_R]
-    own_sin = lax.dynamic_slice_in_dim(sin, own, tok_dev, 0)[:, :D_R]
-
-    def turned(u, way):
-        return u * own_cos + way * jnp.concatenate([u[:, 32:], u[:, :32]], axis=1) * own_sin
-
-    rot = turned(latent[0, :, D_C:].astype(F32), 1.0).astype(BF16)
-    piece = jnp.concatenate([latent[0, :, :D_C], rot, rot], axis=1)
-    rows = lax.all_gather(piece, "grp", axis=0, tiled=True)
-    query_heads = lax.all_to_all(query[0], "grp", split_axis=1, concat_axis=0, tiled=True)
-    lat = jnp.concatenate([from_behind(rows[group_tok - 256 :], "blk", 1), rows], axis=0)
-    grad_query, part = pl.pallas_call(
+    wide = D_C + LANES
+    freq = jnp.asarray(np.tile(freqs_of(D_R), 4)[None])
+    hbm, vmem = pl.BlockSpec(memory_space=pl.ANY), pl.BlockSpec(memory_space=pltpu.VMEM)
+    dma = pltpu.SemaphoreType.DMA
+    grad_query, grad_latent = pl.pallas_call(
         kernel,
         out_shape=(
             jax.ShapeDtypeStruct((group_tok, slots), BF16),
-            jax.ShapeDtypeStruct((key_rows, D_C + LANES), F32),
+            jax.ShapeDtypeStruct((tok_dev, D_C + D_R), BF16),
         ),
-        in_specs=[pl.BlockSpec(memory_space=pltpu.VMEM)] * 8,
-        out_specs=(pl.BlockSpec(memory_space=pltpu.VMEM),) * 2,
+        in_specs=[hbm, hbm, vmem, vmem, hbm, hbm, vmem],
+        out_specs=(hbm, vmem),
         scratch_shapes=[
             pltpu.VMEM((group_tok, slots), BF16),
+            pltpu.VMEM((key_rows, wide), BF16),
+            pltpu.VMEM((group_tok, width), BF16),
+            pltpu.VMEM((D_C, width), BF16),
+            pltpu.VMEM((D_C, width), BF16),
+            pltpu.VMEM((group_tok, LANES), F32),
+            pltpu.VMEM((group_tok, LANES), F32),
             pltpu.VMEM((key_rows, slots), BF16),
             pltpu.VMEM((key_rows, LANES), BF16),
             pltpu.VMEM((key_rows, width), BF16),
             pltpu.VMEM((2, 384, 128), F32),
             pltpu.VMEM((key_rows, slots), F32),
             pltpu.VMEM((key_rows, width), F32),
+            pltpu.VMEM((group_tok, slots), BF16),
+            pltpu.VMEM((key_rows, wide), BF16),
+            pltpu.VMEM((256, wide), F32),
+            pltpu.VMEM((7, tok_dev, wide), BF16),
+            pltpu.VMEM((256, wide), BF16),
+            dma((4,)),
+            dma((4,)),
+            dma((7,)),
+            dma((7,)),
+            dma((7,)),
+            dma((7,)),
+            dma((7,)),
+            dma((7,)),
+            dma((2,)),
+            dma((2,)),
         ],
-        compiler_params=pltpu.CompilerParams(vmem_limit_bytes=60 * 1024 * 1024),
-    )(positions, query_heads, grad_out[0], lat, key_up, value_up, cos, sin)
-    part = part[:, : D_C + D_R]
-    own_part = part[256:]
-    returned = from_behind(part[:256], "blk", -1)
-    own_part = jnp.concatenate([own_part[: group_tok - 256], own_part[group_tok - 256 :] + returned], axis=0)
-    summed = lax.psum_scatter(own_part, "grp", scatter_dimension=0, tiled=True)
-    grad_latent = jnp.concatenate([summed[:, :D_C], turned(summed[:, D_C:], -1.0)], axis=1).astype(BF16)
+        compiler_params=pltpu.CompilerParams(
+            vmem_limit_bytes=60 * 1024 * 1024, collective_id=0, has_side_effects=True
+        ),
+    )(query[0], grad_out[0], latent[0], positions, key_up, value_up, freq)
     return (grad_query[None], grad_latent[None])
 
 

time: 228 us -> 114 us (0.50)
  the two profiles are of different devices: /device:TPU:6 before, /device:TPU:1 now
where the time goes in v2:
time: 114 us
  Pallas kernels  106 us (93%)
  local copies, waits for them, and re-layouts  7.16 us (6%)
    pallas_call x1, Pallas kernels, per_device(): pl.pallas_call(kernel, out_shape=(jax.ShapeDtypeStruct((group_tok, slots)...  106 us
    unnamed x3, local copies, waits for them, and re-layouts  7.16 us

profile of v2, /device:TPU:1, one launch (start us, length us, event | category | flops | bytes accessed | tf_op | source)
XLA Modules:
  0.0 114.0 jit_solution(8314831895632890615)
XLA Ops:
  0.6 1.7 %copy.9 = bf16[1,128,576]{2,1,0:T(8,128)(2,1)} copy(bf16[1,128,576]{1,2,0:T(8,128)(2,1)} %param.8) | data formatting | bytes 294912 | tf_op args[1]
  2.3 106.2 %shard_map.86 = (bf16[1024,1536]{1,0:T(8,128)(2,1)}, bf16[128,576]{1,0:T(8,128)(2,1)}) custom-call(bf16[128,12288]{1,0:T(8,128)(2,1)} %bitcast.5, bf16[1024,1024]{1,0:T(8,128)(2,1)} %bitcast.7, bf16[128,576]{1,0:T(8,128)(2,1)} %bitcast.8, s32[1,1024]{1,0:T(1,128)} %pos.1, bf16[512,1024]{1,0:T(8,128)(2,1)} %key_hbm.1, bf16[512,1024]{1,0:T(8,128)(2,1)} %value_hbm.1, ...), custom_call_target="tpu_custom_call" | custom-call | tf_op jit(solution)/shard_map/pallas_call | solution.py:358
  108.5 1.7 %copy.10 = bf16[1,128,576]{1,2,0:T(8,128)(2,1)} copy(bf16[1,128,576]{2,1,0:T(8,128)(2,1)} %bitcast.9) | data formatting | bytes 294912
  110.2 3.8 %copy.12 = bf16[1,1024,1536]{2,1,0:T(8,128)(2,1)} copy(bf16[1,1024,1536]{2,1,0:T(8,128)(2,1)} %bitcast.6) | data formatting | bytes 6291456

commit v3 on v2

--- a/solution.py
+++ b/solution.py
@@ -198,8 +198,8 @@
     group_tok = qbuf.shape[0]
     ahead, behind = (b + 1) % nb, (b + nb - 1) % nb
 
-    def peer(step, way=1):
-        return ((z + 4 + way * step[0]) % 4) * 2 + (y + step[1]) % 2
+    def peer(step):
+        return ((z + step[0]) % 4) * 2 + (y + step[1]) % 2
 
     def remote(src, dst, send, recv, to_g=None, to_b=None):
         return pltpu.make_async_remote_copy(
@@ -221,8 +221,6 @@
         ),
         pltpu.make_async_copy(gout_hbm, gout, load_sem.at[3]),
     ]
-    for load in loads:
-        load.start()
 
     barrier = pltpu.get_barrier_semaphore()
     for step in STEPS:
@@ -233,22 +231,29 @@
     my = pl.multiple_of(g * 128, 128)
     mine = pl.ds(my, 128)
     fill_tables(my, pos, freq, cos, sin)
-    raw = lat_in[:, D_C:].astype(F32)
-    raw = jnp.concatenate([raw, raw], axis=1)
+
+    def rows_of(gg):
+        return pl.ds(pl.multiple_of(256 + gg * 128, 128), 128)
+
+    raw = lat_in[D_C:, :].astype(F32)
+    raw = jnp.concatenate([raw, raw], axis=0).T
     turned = (raw * cos[mine, :] + swap_halves(raw) * sin[mine, :]).astype(BF16)
-    my_rows = pl.ds(pl.multiple_of(256 + g * 128, 128), 128)
-    lat[my_rows, :D_C] = lat_in[:, :D_C]
-    lat[my_rows, D_C:] = turned
+    lat[rows_of(g), :D_C] = lat_in[:D_C, :].astype(F32).T.astype(BF16)
+    lat[rows_of(g), D_C:] = turned
 
     pl.semaphore_wait(barrier, 9)
-    lat_copies = [
-        remote(lat.at[my_rows, :], lat.at[my_rows, :], lat_send.at[i], lat_recv.at[i], to_g=peer(step))
-        for i, step in enumerate(STEPS)
+
+    def lat_copy(i, of_g, to_g):
+        return remote(lat.at[rows_of(of_g), :], lat.at[rows_of(of_g), :], lat_send.at[i], lat_recv.at[i], to_g=to_g)
+
+    mate = z * 2 + 1 - y
+    first_copies = [lat_copy(0, g, mate)] + [
+        lat_copy(1 + i, g, peer((dz, 0))) for i, dz in enumerate((1, 3, 2))
     ]
-    for copy in lat_copies:
+    for copy in first_copies:
         copy.start()
-    q_copies = [
-        remote(
+    q_copies = {
+        step: remote(
             query.at[:, pl.ds(pl.multiple_of(peer(step) * slots, 128), slots)],
             qbuf.at[mine, :],
             q_send.at[i],
@@ -256,9 +261,15 @@
             to_g=peer(step),
         )
         for i, step in enumerate(STEPS)
-    ]
-    for copy in q_copies:
+    }
+    q_copies[(0, 1)].start()
+    for load in loads:
+        load.start()
+    first_copies[0].wait_recv()
+    second_copies = [lat_copy(4 + i, mate, peer((dz, 0))) for i, dz in enumerate((1, 3, 2))]
+    for copy in second_copies:
         copy.start()
+    lat_copies = first_copies + second_copies
 
     dkacc[...] = jnp.zeros_like(dkacc)
     dvacc[...] = jnp.zeros_like(dvacc)
@@ -270,64 +281,84 @@
     lax.fori_loop(0, group_tok // 128, table, 0)
 
     for copy in lat_copies:
+        copy.wait_send()
+    for copy in lat_copies[1:]:
         copy.wait_recv()
     halo = remote(lat.at[pl.ds(group_tok, 256), :], lat.at[pl.ds(0, 256), :], h_send.at[0], h_recv.at[0], to_b=ahead)
     halo.start()
+    for step in ((1, 0), (3, 0), (1, 1), (3, 1)):
+        q_copies[step].start()
     loads[0].wait()
     loads[1].wait()
 
-    def prepare(j, _):
-        project_rows(pl.multiple_of(j * 256, 256), 256, lat, key_up, value_up, kslot, krot, values)
-        return 0
-
-    lax.fori_loop(1, group_tok // 256 + 1, prepare, 0)
-    halo.wait_recv()
-    prepare(0, 0)
+    project_rows(256, group_tok, lat, key_up, value_up, kslot, krot, values)
     loads[2].wait()
     loads[3].wait()
+    halo.wait_recv()
+    project_rows(0, 256, lat, key_up, value_up, kslot, krot, values)
+
+    back = remote(sbuf.at[0:256, :], hbuf, h_send.at[1], h_recv.at[1], to_b=behind)
+    g_copies = []
+
+    def return_halo():
+        total, turn = gather_back(0, 256, key_up, value_up, dkacc, dvacc)
+        sbuf[0:256, :D_C] = total.astype(BF16)
+        sbuf[0:256, D_C:] = turn.astype(BF16)
+        back.start()
+
+    def send_back(way):
+        block = (z + way) % 4
+        first = pl.multiple_of(256 + block * 256, 256)
+        total, turn = gather_back(first, 256, key_up, value_up, dkacc, dvacc)
+        if way:
+            sbuf[pl.ds(first, 256), :D_C] = total.astype(BF16)
+            sbuf[pl.ds(first, 256), D_C:] = turn.astype(BF16)
+        else:
+            own[:, :D_C] = total
+            own[:, D_C:] = turn
+
+        @pl.when(block == 3)
+        def _():
+            back.wait_recv()
+            if way:
+                sbuf[pl.ds(first, 256), :] = (sbuf[pl.ds(first, 256), :].astype(F32) + hbuf[...].astype(F32)).astype(BF16)
+            else:
+                own[...] += hbuf[...].astype(F32)
+
+        if not way:
+            row = pl.multiple_of((1 - y) * 128, 128)
+            sbuf[pl.ds(pl.multiple_of(first + row, 128), 128), :] = own[pl.ds(row, 128), :].astype(BF16)
+        for i, step in enumerate(STEPS):
+            if step[0] == way:
+                copy = remote(sbuf.at[rows_of(peer(step)), :], rbuf.at[i], g_send.at[i], g_recv.at[i], to_g=peer(step))
+                copy.start()
+                g_copies.append(copy)
 
     stores = []
-    for i, (way, arrivals) in enumerate(((0, (0,)), (-1, (1, 2)), (1, (3, 4)), (2, (5, 6)))):
-        for a in arrivals:
-            q_copies[a].wait_recv()
-        first = pl.multiple_of(((z + 4 + way) % 4) * 256, 256)
+    for i, way in enumerate((0, 3, 1, 2)):
+        block = (z + way) % 4
+        for dy in (0, 1):
+            step = ((4 - way) % 4, dy)
+            if step in q_copies:
+                q_copies[step].wait_recv()
+        first = pl.multiple_of(block * 256, 256)
         turn_queries(first, 256, qbuf, cos, sin)
         fill_bias(first, pos, bias)
         attend(first, qbuf, gout, kslot, krot, values, bias, cos, sin, dq, dkacc, dvacc)
         store = pltpu.make_async_copy(dq.at[pl.ds(first, 256), :], dq_hbm.at[pl.ds(first, 256), :], store_sem.at[i])
         store.start()
         stores.append(store)
-
-    total, turn = gather_back(0, 256, key_up, value_up, dkacc, dvacc)
-    sbuf[0:256, :D_C] = total.astype(BF16)
-    sbuf[0:256, D_C:] = turn.astype(BF16)
-    back = remote(sbuf.at[0:256, :], hbuf, h_send.at[1], h_recv.at[1], to_b=behind)
-    back.start()
-
-    g_copies = []
-    for way in (2, 1, 3, 0):
-        block = (z + way) % 4
-        first = pl.multiple_of(256 + block * 256, 256)
-        total, turn = gather_back(first, 256, key_up, value_up, dkacc, dvacc)
-        own[:, :D_C] = total
-        own[:, D_C:] = turn
-
-        @pl.when(block == 3)
-        def _():
-            back.wait_recv()
-            own[...] += hbuf[...].astype(F32)
-
-        if way:
-            sbuf[pl.ds(first, 256), :] = own[...].astype(BF16)
-        else:
-            first = pl.multiple_of(first + (1 - y) * 128, 128)
-            sbuf[pl.ds(first, 128), :] = own[pl.ds(pl.multiple_of((1 - y) * 128, 128), 128), :].astype(BF16)
-        for i, step in enumerate(STEPS):
-            if step[0] == way:
-                rows = pl.ds(pl.multiple_of(256 + peer(step) * 128, 128), 128)
-                copy = remote(sbuf.at[rows, :], rbuf.at[i], g_send.at[i], g_recv.at[i], to_g=peer(step))
-                copy.start()
-                g_copies.append(copy)
+        if i == 0:
+            q_copies[(2, 0)].start()
+            q_copies[(2, 1)].start()
+        pl.when(block == 0)(return_halo)
+        if i == 1:
+            send_back(3)
+        if i == 2:
+            send_back(0)
+        if i == 3:
+            send_back(2)
+            send_back(1)
 
     total = own[pl.ds(pl.multiple_of(y * 128, 128), 128), :]
     for copy in g_copies:
@@ -336,10 +367,10 @@
         total = total + rbuf[i].astype(F32)
     turn = total[:, D_C:]
     turn = turn * cos[mine, :] - swap_halves(turn) * sin[mine, :]
-    glat[:, :D_C] = total[:, :D_C].astype(BF16)
-    glat[:, D_C:] = turn[:, :D_R].astype(BF16)
-
-    for copy in lat_copies + q_copies + g_copies + [halo, back]:
+    glat[:D_C, :] = total[:, :D_C].T.astype(BF16)
+    glat[D_C:, :] = turn.T[:D_R, :].astype(BF16)
+
+    for copy in list(q_copies.values()) + g_copies + [halo, back]:
         copy.wait_send()
     for store in stores:
         store.wait()
@@ -359,7 +390,7 @@
         kernel,
         out_shape=(
             jax.ShapeDtypeStruct((group_tok, slots), BF16),
-            jax.ShapeDtypeStruct((tok_dev, D_C + D_R), BF16),
+            jax.ShapeDtypeStruct((D_C + D_R, tok_dev), BF16),
         ),
         in_specs=[hbm, hbm, vmem, vmem, hbm, hbm, vmem],
         out_specs=(hbm, vmem),
@@ -396,8 +427,8 @@
         compiler_params=pltpu.CompilerParams(
             vmem_limit_bytes=60 * 1024 * 1024, collective_id=0, has_side_effects=True
         ),
-    )(query[0], grad_out[0], latent[0], positions, key_up, value_up, freq)
-    return (grad_query[None], grad_latent[None])
+    )(query[0], grad_out[0], latent[0].T, positions, key_up, value_up, freq)
+    return (grad_query[None], grad_latent.T[None])
 
 
 def solution(mesh):

time: 114 us -> 92.5 us (0.81)
  the two profiles are of different devices: /device:TPU:1 before, /device:TPU:6 now
where the time goes in v3:
time: 92.5 us; the launch traced here: 92.4 us
  Pallas kernels  87.3 us (94%)
  local copies, waits for them, and re-layouts  4.46 us (5%)
    pallas_call x1, Pallas kernels, per_device(): pl.pallas_call(kernel, out_shape=(jax.ShapeDtypeStruct((group_tok, slots)...  87.3 us
    unnamed x4, local copies, waits for them, and re-layouts  4.46 us

profile of v3, /device:TPU:6, one launch (start us, length us, event | category | flops | bytes accessed | tf_op | source)
XLA Modules:
  0.0 92.4 jit_solution(1905190974864449760)
XLA Ops:
  0.6 87.3 %shard_map.86 = (bf16[1024,1536]{1,0:T(8,128)(2,1)}, bf16[576,128]{1,0:T(8,128)(2,1)}) custom-call(bf16[128,12288]{1,0:T(8,128)(2,1)} %bitcast.9, bf16[1024,1024]{1,0:T(8,128)(2,1)} %bitcast.11, bf16[576,128]{1,0:T(8,128)(2,1)} %bitcast.13, s32[1,1024]{1,0:T(1,128)} %pos.1, bf16[512,1024]{1,0:T(8,128)(2,1)} %key_hbm.1, bf16[512,1024]{1,0:T(8,128)(2,1)} %value_hbm.1, ...), custom_call_target="tpu_custom_call" | custom-call | tf_op jit(solution)/shard_map/pallas_call | solution.py:389
  87.9 0.0 copy-start
  87.9 3.8 %copy.11 = bf16[1,1024,1536]{2,1,0:T(8,128)(2,1)} copy(bf16[1,1024,1536]{2,1,0:T(8,128)(2,1)} %bitcast.10) | data formatting | bytes 6291456
  91.7 0.0 copy-done
  91.7 0.7 copy.12
Async XLA Ops:
  87.9 3.8 %copy-start = (bf16[576,128]{1,0:T(8,128)(2,1)S(1)}, bf16[576,128]{1,0:T(8,128)(2,1)}, u32[]{:S(2)}) copy-start(bf16[576,128]{1,0:T(8,128)(2,1)} %get-tuple-element.5) | copy-start | bytes 442372

commit v4 on v3

--- a/solution.py
+++ b/solution.py
@@ -82,7 +82,7 @@
     lax.fori_loop(0, key_up.shape[1] // 256, pair, 0)
 
 
-def turn_queries(first, rows, qbuf, cos, sin):
+def turn_queries(first, rows, pairs, qbuf, cos, sin):
     span = pl.ds(first, rows)
     low = lane_of(rows) < 64
     c, s = cos[span, :], sin[span, :]
@@ -97,7 +97,7 @@
         qbuf[span, at2] = jnp.where(low, two, r).astype(BF16)
         return 0
 
-    lax.fori_loop(0, qbuf.shape[1] // 384, pair, 0)
+    lax.fori_loop(*pairs, pair, 0)
 
 
 def fill_bias(first, pos, bias):
@@ -129,7 +129,7 @@
     return jnp.concatenate(probs, axis=1), jnp.concatenate(grads, axis=1)
 
 
-def attend(first, qbuf, gout, kslot, krot, values, bias, cos, sin, dq, dkacc, dvacc):
+def attend(first, pairs, qbuf, gout, kslot, krot, values, bias, cos, sin, dq, dkacc, dvacc):
     qs, ks = pl.ds(first, 256), pl.ds(first, 512)
 
     def pair(p, _):
@@ -163,7 +163,7 @@
         dq[qs, pl.ds(pl.multiple_of(s0 + 256, 128), 128)] = jnp.where(low, two, r).astype(BF16)
         return 0
 
-    lax.fori_loop(0, qbuf.shape[1] // 384, pair, 0)
+    lax.fori_loop(*pairs, pair, 0)
 
 
 def gather_back(first, rows, key_up, value_up, dkacc, dvacc):
@@ -188,8 +188,8 @@
 
 def kernel(
     query, gout_hbm, lat_in, pos, key_hbm, value_hbm, freq, dq_hbm, glat,
-    qbuf, lat, gout, key_up, value_up, cos, sin, kslot, krot, values, bias, dkacc, dvacc, dq, sbuf, own, rbuf, hbuf,
-    load_sem, store_sem, lat_send, lat_recv, q_send, q_recv, g_send, g_recv, h_send, h_recv,
+    qbuf, lat, gout, key_up, value_up, cos, sin, kslot, krot, values, bias, dkacc, dvacc, dq, sbuf, own, keep, mbuf, rbuf, hbuf,
+    load_sem, store_sem, lat_send, lat_recv, q_send, q_recv, m_send, m_recv, g_send, g_recv, h_send, h_recv,
 ):
     g, b = lax.axis_index("grp"), lax.axis_index("blk")
     nb = lax.axis_size("blk")
@@ -243,33 +243,42 @@
 
     pl.semaphore_wait(barrier, 9)
 
-    def lat_copy(i, of_g, to_g):
-        return remote(lat.at[rows_of(of_g), :], lat.at[rows_of(of_g), :], lat_send.at[i], lat_recv.at[i], to_g=to_g)
+    def lat_copy(i, of_g, to_g, begin=0, rows=128):
+        span = pl.ds(pl.multiple_of(256 + of_g * 128 + begin, 64), rows)
+        return remote(lat.at[span, :], lat.at[span, :], lat_send.at[i], lat_recv.at[i], to_g=to_g)
 
     mate = z * 2 + 1 - y
-    first_copies = [lat_copy(0, g, mate)] + [
-        lat_copy(1 + i, g, peer((dz, 0))) for i, dz in enumerate((1, 3, 2))
-    ]
-    for copy in first_copies:
+    hops = (1, 3, 2)
+    lat_copies = [lat_copy(0, g, mate)] + [lat_copy(1 + i, g, peer((dz, 0))) for i, dz in enumerate(hops)]
+    for copy in lat_copies:
         copy.start()
-    q_copies = {
-        step: remote(
-            query.at[:, pl.ds(pl.multiple_of(peer(step) * slots, 128), slots)],
-            qbuf.at[mine, :],
-            q_send.at[i],
-            q_recv.at[i],
-            to_g=peer(step),
-        )
-        for i, step in enumerate(STEPS)
-    }
-    q_copies[(0, 1)].start()
     for load in loads:
         load.start()
-    first_copies[0].wait_recv()
-    second_copies = [lat_copy(4 + i, mate, peer((dz, 0))) for i, dz in enumerate((1, 3, 2))]
-    for copy in second_copies:
+    lat_copies[0].wait_recv()
+    for i, dz in enumerate(hops):
+        copy = lat_copy(4 + i, mate, peer((dz, 0)), 64, 64)
         copy.start()
-    lat_copies = first_copies + second_copies
+        lat_copies.append(copy)
+    for i, dz in enumerate(hops):
+        lat_copies[1 + i].wait_recv()
+        copy = lat_copy(7 + i, ((z + 4 - dz) % 4) * 2 + y, mate, 0, 64)
+        copy.start()
+        lat_copies.append(copy)
+
+    half = slots // 2
+    q_copies = {}
+    for dz, dy in STEPS:
+        for part in (0, 1) if dz == 2 else (None,):
+            n = len(q_copies)
+            begin, count = (0, slots) if part is None else (part * half, half)
+            q_copies[(dz, dy, part)] = remote(
+                query.at[:, pl.ds(pl.multiple_of(peer((dz, dy)) * slots + begin, 128), count)],
+                qbuf.at[mine, begin : begin + count],
+                q_send.at[n],
+                q_recv.at[n],
+                to_g=peer((dz, dy)),
+            )
+    q_copies[(0, 1, None)].start()
 
     dkacc[...] = jnp.zeros_like(dkacc)
     dvacc[...] = jnp.zeros_like(dvacc)
@@ -282,12 +291,14 @@
 
     for copy in lat_copies:
         copy.wait_send()
-    for copy in lat_copies[1:]:
+    q_copies[(1, 0, None)].start()
+    q_copies[(3, 0, None)].start()
+    for copy in lat_copies[4:]:
         copy.wait_recv()
     halo = remote(lat.at[pl.ds(group_tok, 256), :], lat.at[pl.ds(0, 256), :], h_send.at[0], h_recv.at[0], to_b=ahead)
     halo.start()
-    for step in ((1, 0), (3, 0), (1, 1), (3, 1)):
-        q_copies[step].start()
+    q_copies[(1, 1, None)].start()
+    q_copies[(3, 1, None)].start()
     loads[0].wait()
     loads[1].wait()
 
@@ -298,79 +309,85 @@
     project_rows(0, 256, lat, key_up, value_up, kslot, krot, values)
 
     back = remote(sbuf.at[0:256, :], hbuf, h_send.at[1], h_recv.at[1], to_b=behind)
-    g_copies = []
-
     def return_halo():
         total, turn = gather_back(0, 256, key_up, value_up, dkacc, dvacc)
         sbuf[0:256, :D_C] = total.astype(BF16)
         sbuf[0:256, D_C:] = turn.astype(BF16)
         back.start()
 
-    def send_back(way):
+    mate_copies = {}
+
+    def send_mate(way):
         block = (z + way) % 4
-        first = pl.multiple_of(256 + block * 256, 256)
-        total, turn = gather_back(first, 256, key_up, value_up, dkacc, dvacc)
-        if way:
-            sbuf[pl.ds(first, 256), :D_C] = total.astype(BF16)
-            sbuf[pl.ds(first, 256), D_C:] = turn.astype(BF16)
-        else:
-            own[:, :D_C] = total
-            own[:, D_C:] = turn
+        total, turn = gather_back(pl.multiple_of(256 + block * 256, 256), 256, key_up, value_up, dkacc, dvacc)
+        own[:, :D_C] = total
+        own[:, D_C:] = turn
 
         @pl.when(block == 3)
         def _():
             back.wait_recv()
-            if way:
-                sbuf[pl.ds(first, 256), :] = (sbuf[pl.ds(first, 256), :].astype(F32) + hbuf[...].astype(F32)).astype(BF16)
-            else:
-                own[...] += hbuf[...].astype(F32)
-
-        if not way:
-            row = pl.multiple_of((1 - y) * 128, 128)
-            sbuf[pl.ds(pl.multiple_of(first + row, 128), 128), :] = own[pl.ds(row, 128), :].astype(BF16)
-        for i, step in enumerate(STEPS):
-            if step[0] == way:
-                copy = remote(sbuf.at[rows_of(peer(step)), :], rbuf.at[i], g_send.at[i], g_recv.at[i], to_g=peer(step))
-                copy.start()
-                g_copies.append(copy)
+            own[...] += hbuf[...].astype(F32)
+
+        keep[way] = own[pl.ds(pl.multiple_of(y * 128, 128), 128), :]
+        span = rows_of(block * 2 + 1 - y)
+        sbuf[span, :] = own[pl.ds(pl.multiple_of((1 - y) * 128, 128), 128), :].astype(BF16)
+        mate_copies[way] = remote(sbuf.at[span, :], mbuf.at[way], m_send.at[way], m_recv.at[way], to_g=mate)
+        mate_copies[way].start()
+
+    z_copies = []
+
+    def send_on(way):
+        span = rows_of(((z + way) % 4) * 2 + y)
+        mate_copies[way].wait_recv()
+        sbuf[span, :] = (keep[way] + mbuf[way].astype(F32)).astype(BF16)
+        copy = remote(sbuf.at[span, :], rbuf.at[way - 1], g_send.at[way - 1], g_recv.at[way - 1], to_g=peer((way, 0)))
+        copy.start()
+        z_copies.append(copy)
 
     stores = []
     for i, way in enumerate((0, 3, 1, 2)):
         block = (z + way) % 4
-        for dy in (0, 1):
-            step = ((4 - way) % 4, dy)
-            if step in q_copies:
-                q_copies[step].wait_recv()
         first = pl.multiple_of(block * 256, 256)
-        turn_queries(first, 256, qbuf, cos, sin)
-        fill_bias(first, pos, bias)
-        attend(first, qbuf, gout, kslot, krot, values, bias, cos, sin, dq, dkacc, dvacc)
+        for part in (0, 1) if way == 2 else (None,):
+            for dy in (0, 1):
+                if way or dy:
+                    q_copies[((4 - way) % 4, dy, part)].wait_recv()
+            if part == 1:
+                send_on(3)
+            pairs = (0, slots // 384) if part is None else (part * slots // 768, (part + 1) * slots // 768)
+            turn_queries(first, 256, pairs, qbuf, cos, sin)
+            if not part:
+                fill_bias(first, pos, bias)
+            attend(first, pairs, qbuf, gout, kslot, krot, values, bias, cos, sin, dq, dkacc, dvacc)
         store = pltpu.make_async_copy(dq.at[pl.ds(first, 256), :], dq_hbm.at[pl.ds(first, 256), :], store_sem.at[i])
         store.start()
         stores.append(store)
-        if i == 0:
-            q_copies[(2, 0)].start()
-            q_copies[(2, 1)].start()
+        if i < 2:
+            q_copies[(2, 0, i)].start()
+            q_copies[(2, 1, i)].start()
         pl.when(block == 0)(return_halo)
         if i == 1:
-            send_back(3)
+            send_mate(3)
         if i == 2:
-            send_back(0)
+            send_mate(0)
         if i == 3:
-            send_back(2)
-            send_back(1)
-
-    total = own[pl.ds(pl.multiple_of(y * 128, 128), 128), :]
-    for copy in g_copies:
+            send_mate(2)
+            send_mate(1)
+            send_on(2)
+            send_on(1)
+
+    mate_copies[0].wait_recv()
+    total = keep[0] + mbuf[0].astype(F32)
+    for copy in z_copies:
         copy.wait_recv()
-    for i in range(len(STEPS)):
+    for i in range(3):
         total = total + rbuf[i].astype(F32)
     turn = total[:, D_C:]
     turn = turn * cos[mine, :] - swap_halves(turn) * sin[mine, :]
     glat[:D_C, :] = total[:, :D_C].T.astype(BF16)
     glat[D_C:, :] = turn.T[:D_R, :].astype(BF16)
 
-    for copy in list(q_copies.values()) + g_copies + [halo, back]:
+    for copy in [*q_copies.values(), *mate_copies.values(), *z_copies, halo, back]:
         copy.wait_send()
     for store in stores:
         store.wait()
@@ -411,16 +428,20 @@
             pltpu.VMEM((group_tok, slots), BF16),
             pltpu.VMEM((key_rows, wide), BF16),
             pltpu.VMEM((256, wide), F32),
-            pltpu.VMEM((7, tok_dev, wide), BF16),
+            pltpu.VMEM((4, tok_dev, wide), F32),
+            pltpu.VMEM((4, tok_dev, wide), BF16),
+            pltpu.VMEM((3, tok_dev, wide), BF16),
             pltpu.VMEM((256, wide), BF16),
             dma((4,)),
             dma((4,)),
-            dma((7,)),
-            dma((7,)),
-            dma((7,)),
-            dma((7,)),
-            dma((7,)),
-            dma((7,)),
+            dma((10,)),
+            dma((10,)),
+            dma((9,)),
+            dma((9,)),
+            dma((4,)),
+            dma((4,)),
+            dma((3,)),
+            dma((3,)),
             dma((2,)),
             dma((2,)),
         ],

time: 92.5 us -> 98 us (1.059); the launches traced: 92.4 us -> 96.7 us
  Pallas kernels: 87.3 us -> 91.5 us
    pallas_call x1, Pallas kernels: 87.3 us -> 91.5 us  [per_device(): pl.pallas_call(kernel, out_shape=(jax.ShapeDtypeStruct((group_tok, slots)...]
where the time goes in v4:
time: 98 us; the launch traced here: 96.7 us
  Pallas kernels  91.5 us (93%)
  local copies, waits for them, and re-layouts  4.46 us (5%)
    pallas_call x1, Pallas kernels, per_device(): pl.pallas_call(kernel, out_shape=(jax.ShapeDtypeStruct((group_tok, slots)...  91.5 us
    unnamed x4, local copies, waits for them, and re-layouts  4.46 us

profile of v4, /device:TPU:6, one launch (start us, length us, event | category | flops | bytes accessed | tf_op | source)
XLA Modules:
  0.0 96.7 jit_solution(17057099314875199593)
XLA Ops:
  0.6 91.5 %shard_map.86 = (bf16[1024,1536]{1,0:T(8,128)(2,1)}, bf16[576,128]{1,0:T(8,128)(2,1)}) custom-call(bf16[128,12288]{1,0:T(8,128)(2,1)} %bitcast.9, bf16[1024,1024]{1,0:T(8,128)(2,1)} %bitcast.11, bf16[576,128]{1,0:T(8,128)(2,1)} %bitcast.13, s32[1,1024]{1,0:T(1,128)} %pos.1, bf16[512,1024]{1,0:T(8,128)(2,1)} %key_hbm.1, bf16[512,1024]{1,0:T(8,128)(2,1)} %value_hbm.1, ...), custom_call_target="tpu_custom_call" | custom-call | tf_op jit(solution)/shard_map/pallas_call | solution.py:406
  92.2 0.0 copy-start
  92.2 3.8 %copy.11 = bf16[1,1024,1536]{2,1,0:T(8,128)(2,1)} copy(bf16[1,1024,1536]{2,1,0:T(8,128)(2,1)} %bitcast.10) | data formatting | bytes 6291456
  96.0 0.0 copy-done
  96.0 0.7 copy.12
Async XLA Ops:
  92.2 3.8 %copy-start = (bf16[576,128]{1,0:T(8,128)(2,1)S(1)}, bf16[576,128]{1,0:T(8,128)(2,1)}, u32[]{:S(2)}) copy-start(bf16[576,128]{1,0:T(8,128)(2,1)} %get-tuple-element.5) | copy-start | bytes 442372

commit v5 on v3

--- a/solution.py
+++ b/solution.py
@@ -82,7 +82,7 @@
     lax.fori_loop(0, key_up.shape[1] // 256, pair, 0)
 
 
-def turn_queries(first, rows, qbuf, cos, sin):
+def turn_queries(first, rows, pairs, qbuf, cos, sin):
     span = pl.ds(first, rows)
     low = lane_of(rows) < 64
     c, s = cos[span, :], sin[span, :]
@@ -97,7 +97,7 @@
         qbuf[span, at2] = jnp.where(low, two, r).astype(BF16)
         return 0
 
-    lax.fori_loop(0, qbuf.shape[1] // 384, pair, 0)
+    lax.fori_loop(*pairs, pair, 0)
 
 
 def fill_bias(first, pos, bias):
@@ -129,7 +129,7 @@
     return jnp.concatenate(probs, axis=1), jnp.concatenate(grads, axis=1)
 
 
-def attend(first, qbuf, gout, kslot, krot, values, bias, cos, sin, dq, dkacc, dvacc):
+def attend(first, pairs, qbuf, gout, kslot, krot, values, bias, cos, sin, dq, dkacc, dvacc):
     qs, ks = pl.ds(first, 256), pl.ds(first, 512)
 
     def pair(p, _):
@@ -163,7 +163,7 @@
         dq[qs, pl.ds(pl.multiple_of(s0 + 256, 128), 128)] = jnp.where(low, two, r).astype(BF16)
         return 0
 
-    lax.fori_loop(0, qbuf.shape[1] // 384, pair, 0)
+    lax.fori_loop(*pairs, pair, 0)
 
 
 def gather_back(first, rows, key_up, value_up, dkacc, dvacc):
@@ -252,17 +252,20 @@
     ]
     for copy in first_copies:
         copy.start()
-    q_copies = {
-        step: remote(
-            query.at[:, pl.ds(pl.multiple_of(peer(step) * slots, 128), slots)],
-            qbuf.at[mine, :],
-            q_send.at[i],
-            q_recv.at[i],
-            to_g=peer(step),
-        )
-        for i, step in enumerate(STEPS)
-    }
-    q_copies[(0, 1)].start()
+    half = slots // 2
+    q_copies = {}
+    for dz, dy in STEPS:
+        for part in (0, 1) if dz == 2 else (None,):
+            n = len(q_copies)
+            begin, count = (0, slots) if part is None else (part * half, half)
+            q_copies[(dz, dy, part)] = remote(
+                query.at[:, pl.ds(pl.multiple_of(peer((dz, dy)) * slots + begin, 128), count)],
+                qbuf.at[mine, begin : begin + count],
+                q_send.at[n],
+                q_recv.at[n],
+                to_g=peer((dz, dy)),
+            )
+    q_copies[(0, 1, None)].start()
     for load in loads:
         load.start()
     first_copies[0].wait_recv()
@@ -287,7 +290,7 @@
     halo = remote(lat.at[pl.ds(group_tok, 256), :], lat.at[pl.ds(0, 256), :], h_send.at[0], h_recv.at[0], to_b=ahead)
     halo.start()
     for step in ((1, 0), (3, 0), (1, 1), (3, 1)):
-        q_copies[step].start()
+        q_copies[(*step, None)].start()
     loads[0].wait()
     loads[1].wait()
 
@@ -337,20 +340,23 @@
     stores = []
     for i, way in enumerate((0, 3, 1, 2)):
         block = (z + way) % 4
-        for dy in (0, 1):
-            step = ((4 - way) % 4, dy)
-            if step in q_copies:
-                q_copies[step].wait_recv()
         first = pl.multiple_of(block * 256, 256)
-        turn_queries(first, 256, qbuf, cos, sin)
-        fill_bias(first, pos, bias)
-        attend(first, qbuf, gout, kslot, krot, values, bias, cos, sin, dq, dkacc, dvacc)
+        for part in (0, 1) if way == 2 else (None,):
+            for dy in (0, 1):
+                if way or dy:
+                    q_copies[((4 - way) % 4, dy, part)].wait_recv()
+            pairs = (0, slots // 384) if part is None else (part * slots // 768, (part + 1) * slots // 768)
+            turn_queries(first, 256, pairs, qbuf, cos, sin)
+            if not part:
+                fill_bias(first, pos, bias)
+            attend(first, pairs, qbuf, gout, kslot, krot, values, bias, cos, sin, dq, dkacc, dvacc)
         store = pltpu.make_async_copy(dq.at[pl.ds(first, 256), :], dq_hbm.at[pl.ds(first, 256), :], store_sem.at[i])
         store.start()
         stores.append(store)
         if i == 0:
-            q_copies[(2, 0)].start()
-            q_copies[(2, 1)].start()
+            for part in (0, 1):
+                q_copies[(2, 0, part)].start()
+                q_copies[(2, 1, part)].start()
         pl.when(block == 0)(return_halo)
         if i == 1:
             send_back(3)
@@ -417,8 +423,8 @@
             dma((4,)),
             dma((7,)),
             dma((7,)),
-            dma((7,)),
-            dma((7,)),
+            dma((9,)),
+            dma((9,)),
             dma((7,)),
             dma((7,)),
             dma((2,)),

time: 92.5 us -> 90.3 us (0.976)
  Pallas kernels: 87.3 us -> 85 us
    pallas_call x1, Pallas kernels: 87.3 us -> 85 us  [per_device(): pl.pallas_call(kernel, out_shape=(jax.ShapeDtypeStruct((group_tok, slots)...]
where the time goes in v5:
time: 90.3 us; the launch traced here: 90.1 us
  Pallas kernels  85 us (94%)
  local copies, waits for them, and re-layouts  4.46 us (5%)
    pallas_call x1, Pallas kernels, per_device(): pl.pallas_call(kernel, out_shape=(jax.ShapeDtypeStruct((group_tok, slots)...  85 us
    unnamed x4, local copies, waits for them, and re-layouts  4.46 us

profile of v5, /device:TPU:6, one launch (start us, length us, event | category | flops | bytes accessed | tf_op | source)
XLA Modules:
  0.0 90.1 jit_solution(6271264759615472412)
XLA Ops:
  0.6 85.0 %shard_map.86 = (bf16[1024,1536]{1,0:T(8,128)(2,1)}, bf16[576,128]{1,0:T(8,128)(2,1)}) custom-call(bf16[128,12288]{1,0:T(8,128)(2,1)} %bitcast.9, bf16[1024,1024]{1,0:T(8,128)(2,1)} %bitcast.11, bf16[576,128]{1,0:T(8,128)(2,1)} %bitcast.13, s32[1,1024]{1,0:T(1,128)} %pos.1, bf16[512,1024]{1,0:T(8,128)(2,1)} %key_hbm.1, bf16[512,1024]{1,0:T(8,128)(2,1)} %value_hbm.1, ...), custom_call_target="tpu_custom_call" | custom-call | tf_op jit(solution)/shard_map/pallas_call | solution.py:395
  85.7 0.0 copy-start
  85.7 3.8 %copy.11 = bf16[1,1024,1536]{2,1,0:T(8,128)(2,1)} copy(bf16[1,1024,1536]{2,1,0:T(8,128)(2,1)} %bitcast.10) | data formatting | bytes 6291456
  89.5 0.0 copy-done
  89.5 0.7 copy.12
Async XLA Ops:
  85.7 3.8 %copy-start = (bf16[576,128]{1,0:T(8,128)(2,1)S(1)}, bf16[576,128]{1,0:T(8,128)(2,1)}, u32[]{:S(2)}) copy-start(bf16[576,128]{1,0:T(8,128)(2,1)} %get-tuple-element.5) | copy-start | bytes 442372

commit v6 on v5

--- a/solution.py
+++ b/solution.py
@@ -116,11 +116,12 @@
         s = scores[rows, cols] + bias[half]
         d = dprob[rows, cols]
         top = jnp.max(s, axis=0, keepdims=True)
-        e = jnp.exp((s - top) * SCALING)
+        e = jnp.exp2((s - top) * (SCALING * math.log2(math.e)))
         total = jnp.sum(e, axis=0, keepdims=True)
-        delta = jnp.sum(e * d, axis=0, keepdims=True) / total
-        prob = e * (1.0 / total)
-        grad = (prob * (d - delta) * SCALING).astype(BF16)
+        share = 1.0 / total
+        delta = jnp.sum(e * d, axis=0, keepdims=True) * share
+        prob = e * share
+        grad = (prob * ((d - delta) * SCALING)).astype(BF16)
         prob = prob.astype(BF16)
         none = jnp.zeros((128, 128), BF16)
         order = (lambda x: [x, none]) if half == 0 else (lambda x: [none, x])
@@ -163,7 +164,7 @@
         dq[qs, pl.ds(pl.multiple_of(s0 + 256, 128), 128)] = jnp.where(low, two, r).astype(BF16)
         return 0
 
-    lax.fori_loop(*pairs, pair, 0)
+    lax.fori_loop(*pairs, pair, 0, unroll=2)
 
 
 def gather_back(first, rows, key_up, value_up, dkacc, dvacc):
@@ -357,13 +358,15 @@
             for part in (0, 1):
                 q_copies[(2, 0, part)].start()
                 q_copies[(2, 1, part)].start()
-        pl.when(block == 0)(return_halo)
+        if i < 3:
+            pl.when(block == 0)(return_halo)
         if i == 1:
             send_back(3)
         if i == 2:
             send_back(0)
         if i == 3:
             send_back(2)
+            pl.when(block == 0)(return_halo)
             send_back(1)
 
     total = own[pl.ds(pl.multiple_of(y * 128, 128), 128), :]

time: 90.3 us -> 89.1 us (0.987)
  Pallas kernels: 85 us -> 83.9 us
    pallas_call x1, Pallas kernels: 85 us -> 83.9 us  [per_device(): pl.pallas_call(kernel, out_shape=(jax.ShapeDtypeStruct((group_tok, slots)...]
where the time goes in v6:
time: 89.1 us; the launch traced here: 89 us
  Pallas kernels  83.9 us (94%)
  local copies, waits for them, and re-layouts  4.46 us (5%)
    pallas_call x1, Pallas kernels, per_device(): pl.pallas_call(kernel, out_shape=(jax.ShapeDtypeStruct((group_tok, slots)...  83.9 us
    unnamed x4, local copies, waits for them, and re-layouts  4.46 us

profile of v6, /device:TPU:6, one launch (start us, length us, event | category | flops | bytes accessed | tf_op | source)
XLA Modules:
  0.0 89.0 jit_solution(15396606956828886688)
XLA Ops:
  0.6 83.9 %shard_map.86 = (bf16[1024,1536]{1,0:T(8,128)(2,1)}, bf16[576,128]{1,0:T(8,128)(2,1)}) custom-call(bf16[128,12288]{1,0:T(8,128)(2,1)} %bitcast.9, bf16[1024,1024]{1,0:T(8,128)(2,1)} %bitcast.11, bf16[576,128]{1,0:T(8,128)(2,1)} %bitcast.13, s32[1,1024]{1,0:T(1,128)} %pos.1, bf16[512,1024]{1,0:T(8,128)(2,1)} %key_hbm.1, bf16[512,1024]{1,0:T(8,128)(2,1)} %value_hbm.1, ...), custom_call_target="tpu_custom_call" | custom-call | tf_op jit(solution)/shard_map/pallas_call | solution.py:398
  84.5 0.0 copy-start
  84.5 3.8 %copy.11 = bf16[1,1024,1536]{2,1,0:T(8,128)(2,1)} copy(bf16[1,1024,1536]{2,1,0:T(8,128)(2,1)} %bitcast.10) | data formatting | bytes 6291456
  88.3 0.0 copy-done
  88.3 0.7 copy.12
Async XLA Ops:
  84.5 3.8 %copy-start = (bf16[576,128]{1,0:T(8,128)(2,1)S(1)}, bf16[576,128]{1,0:T(8,128)(2,1)}, u32[]{:S(2)}) copy-start(bf16[576,128]{1,0:T(8,128)(2,1)} %get-tuple-element.5) | copy-start | bytes 442372

commit v7 on v6

--- a/solution.py
+++ b/solution.py
@@ -338,6 +338,27 @@
                 copy.start()
                 g_copies.append(copy)
 
+    def send_back_far():
+        for i, step in enumerate(STEPS):
+            if step[0] != 2:
+                continue
+            to = peer(step)
+            span = rows_of(to)
+            total, turn = gather_back(pl.multiple_of(256 + to * 128, 128), 128, key_up, value_up, dkacc, dvacc)
+            sbuf[span, :D_C] = total.astype(BF16)
+            sbuf[span, D_C:] = turn.astype(BF16)
+
+            @pl.when(to // 2 == 3)
+            def _():
+                if step[1] == 0:
+                    back.wait_recv()
+                part = hbuf[pl.ds(pl.multiple_of((to % 2) * 128, 128), 128), :].astype(F32)
+                sbuf[span, :] = (sbuf[span, :].astype(F32) + part).astype(BF16)
+
+            copy = remote(sbuf.at[span, :], rbuf.at[i], g_send.at[i], g_recv.at[i], to_g=to)
+            copy.start()
+            g_copies.append(copy)
+
     stores = []
     for i, way in enumerate((0, 3, 1, 2)):
         block = (z + way) % 4
@@ -365,7 +386,7 @@
         if i == 2:
             send_back(0)
         if i == 3:
-            send_back(2)
+            send_back_far()
             pl.when(block == 0)(return_halo)
             send_back(1)
 

time: 89.1 us -> 89.4 us (level)
  no operation moved by 1% of the time
where the time goes in v7:
time: 89.4 us; the launch traced here: 89.2 us
  Pallas kernels  84.1 us (94%)
  local copies, waits for them, and re-layouts  4.46 us (5%)
    pallas_call x1, Pallas kernels, per_device(): pl.pallas_call(kernel, out_shape=(jax.ShapeDtypeStruct((group_tok, slots)...  84.1 us
    unnamed x4, local copies, waits for them, and re-layouts  4.46 us

profile of v7, /device:TPU:6, one launch (start us, length us, event | category | flops | bytes accessed | tf_op | source)
XLA Modules:
  0.0 89.2 jit_solution(17569618776470801318)
XLA Ops:
  0.6 84.1 %shard_map.86 = (bf16[1024,1536]{1,0:T(8,128)(2,1)}, bf16[576,128]{1,0:T(8,128)(2,1)}) custom-call(bf16[128,12288]{1,0:T(8,128)(2,1)} %bitcast.9, bf16[1024,1024]{1,0:T(8,128)(2,1)} %bitcast.11, bf16[576,128]{1,0:T(8,128)(2,1)} %bitcast.13, s32[1,1024]{1,0:T(1,128)} %pos.1, bf16[512,1024]{1,0:T(8,128)(2,1)} %key_hbm.1, bf16[512,1024]{1,0:T(8,128)(2,1)} %value_hbm.1, ...), custom_call_target="tpu_custom_call" | custom-call | tf_op jit(solution)/shard_map/pallas_call | solution.py:419
  84.8 0.0 copy-start
  84.8 3.8 %copy.11 = bf16[1,1024,1536]{2,1,0:T(8,128)(2,1)} copy(bf16[1,1024,1536]{2,1,0:T(8,128)(2,1)} %bitcast.10) | data formatting | bytes 6291456
  88.6 0.0 copy-done
  88.6 0.7 copy.12
Async XLA Ops:
  84.8 3.8 %copy-start = (bf16[576,128]{1,0:T(8,128)(2,1)S(1)}, bf16[576,128]{1,0:T(8,128)(2,1)}, u32[]{:S(2)}) copy-start(bf16[576,128]{1,0:T(8,128)(2,1)} %get-tuple-element.5) | copy-start | bytes 442372
